TPU v7x, 256 devices: a whole 4x4x8 slice. The times are simulated.
256 devices in a mesh: loop: 64 (over z, x_lo, y), grp: 4 (over x_hi, core).
Axes of the slice: x: 4 (x_hi: 2, x_lo: 2; x = x_hi * 2 + x_lo), y: 4, z: 8, core: 2. Of those that a mesh axis runs over, the one named last changes fastest.
Arguments:
- image_features: bfloat16 [12288, 1152], P('loop', 'grp'), may hold values from -4.6 to 4.6
- text_features: bfloat16 [12288, 1152], P(('loop', 'grp')), may hold values from -4.6 to 4.6
Outputs:
- image_grad: bfloat16 [12288, 1152], P('loop', 'grp')
- text_grad: bfloat16 [12288, 1152], P(('loop', 'grp'))
All inputs are finite; a program needn't handle non-finite values.
Results may differ from a plain program's by a relative error of at most 0.007.
Values may be sent and summed in bfloat16 or wider, within the bound.
A program may use at most 128 MiB of HBM per device.

v0:
```python
import jax
import jax.numpy as jnp
from jax import lax
from jax.sharding import PartitionSpec as P

LOGIT_SCALE = 16.0
LOGIT_BIAS = -4.0


def padded_2(block, sides, width):
    for axis, dim in sides:
        count = lax.axis_size(axis)
        forward = [(i, i + 1) for i in range(count - 1)]
        forward.append((count - 1, 0))
        backward = [(target, source) for source, target in forward]
        low = lax.ppermute(
            lax.slice_in_dim(block, block.shape[dim] - width, None, axis=dim), axis, forward
        )
        high = lax.ppermute(lax.slice_in_dim(block, 0, width, axis=dim), axis, backward)
        block = jnp.concatenate([low, block, high], axis=dim)
    return block


def pair_scores(left, right):
    return lax.dot_general(
        left, right, (((1,), (1,)), ((), ())), preferred_element_type=jnp.float32
    )


def back_product(loss_coef, rows):
    return lax.dot_general(
        loss_coef, rows, (((0,), (0,)), ((), ())), preferred_element_type=jnp.float32
    )


def on_device(image_features, text_features):
    loop_count = lax.axis_size("loop")
    loop_place = lax.axis_index("loop")
    group_place = lax.axis_index("grp")
    half_loop = loop_count // 2
    whole_image = lax.all_gather(image_features, "grp", axis=1, tiled=True)
    image_values = whole_image.astype(jnp.float32)
    image_scale = lax.rsqrt(jnp.sum(image_values * image_values, axis=-1, keepdims=True) + 1e-06)
    image_low = (image_values * image_scale).astype(jnp.bfloat16)
    text_values = text_features.astype(jnp.float32)
    text_scale = lax.rsqrt(jnp.sum(text_values * text_values, axis=-1, keepdims=True) + 1e-06)
    text_unit = text_values * text_scale
    text_low = text_unit.astype(jnp.bfloat16)
    rows_here = whole_image.shape[0]
    share_rows = text_features.shape[0]
    width = text_features.shape[1]
    row_ids = jnp.arange(rows_here, dtype=jnp.int32)[:, None]
    col_ids = group_place * share_rows + jnp.arange(share_rows, dtype=jnp.int32)[None, :]
    labels = jnp.where(row_ids == col_ids, 1.0, 0.0).astype(jnp.float32)

    def visit(texts, targets, image_dir):
        items = texts.shape[0]
        flat_rows = texts.reshape(items * share_rows, width)
        logits = LOGIT_SCALE * pair_scores(image_low, flat_rows) + LOGIT_BIAS
        loss_coef = (LOGIT_SCALE * (jax.nn.sigmoid(logits) - targets)).astype(jnp.bfloat16)
        image_dir = image_dir + jnp.dot(loss_coef, flat_rows, preferred_element_type=jnp.float32)
        text_parts = back_product(loss_coef, image_low).reshape(items, share_rows, width)
        return (text_parts, image_dir)

    def advance(blocks):
        padded = padded_2(blocks, (("loop", 0),), 1)
        return jnp.stack([padded[3], padded[0]])

    def deposit(grad_store, holder, piece):
        anchor = jnp.zeros((), jnp.int32)
        corner = (holder, anchor, anchor)
        previous = lax.dynamic_slice(grad_store, corner, (1, share_rows, width))
        return lax.dynamic_update_slice(grad_store, previous + piece[None], corner)

    image_dir = jnp.zeros((rows_here, width), jnp.float32)
    own_parts, image_dir = visit(text_low[None], labels, image_dir)
    blocks = jnp.stack([text_low, text_low])
    grad_store = deposit(
        jnp.zeros((loop_count, share_rows, width), jnp.float32), loop_place, own_parts[0]
    )

    def one_step(offset, state_now):
        blocks, grad_store, image_dir = state_now
        blocks = advance(blocks)
        text_parts, image_dir = visit(blocks, 0.0, image_dir)
        grad_store = deposit(grad_store, jnp.mod(loop_place + offset, loop_count), text_parts[0])
        grad_store = deposit(grad_store, jnp.mod(loop_place - offset, loop_count), text_parts[1])
        return (blocks, grad_store, image_dir)

    blocks, grad_store, image_dir = lax.fori_loop(
        1, half_loop, one_step, (blocks, grad_store, image_dir)
    )
    blocks = advance(blocks)
    last_parts, image_dir = visit(blocks[1:], 0.0, image_dir)
    grad_store = deposit(grad_store, jnp.mod(loop_place - half_loop, loop_count), last_parts[0])
    received = lax.all_to_all(grad_store, "loop", split_axis=0, concat_axis=0, tiled=True)
    text_dir = jnp.sum(received, axis=0)
    text_inner = jnp.sum(text_unit * text_dir, axis=-1, keepdims=True)
    text_grad = (text_scale * (text_dir - text_unit * text_inner)).astype(jnp.bfloat16)
    image_share = lax.psum_scatter(image_dir, "grp", scatter_dimension=1, tiled=True)
    unit_share = image_features.astype(jnp.float32) * image_scale
    image_inner = lax.psum(jnp.sum(unit_share * image_share, axis=-1, keepdims=True), "grp")
    image_grad = (image_scale * (image_share - unit_share * image_inner)).astype(jnp.bfloat16)
    return (image_grad, text_grad)


def solution(mesh):
    placed = (P("loop", "grp"), P(("loop", "grp"), None))
    return jax.shard_map(
        on_device,
        mesh=mesh,
        in_specs=placed,
        out_specs=(P("loop", "grp"), P(("loop", "grp"), None)),
        check_vma=False,
    )
```

profile of v0, /device:TPU:16, one launch (start us, length us, event | category | flops | bytes accessed | tf_op | source)
XLA Modules:
  0.0 765.1 jit_solution(2183424875657288904)
XLA Ops:
  8.2 9.1 %all_gather.3 = bf16[192,1152]{0,1:T(8,128)(2,1)S(1)} all-gather(bf16[192,288]{0,1:T(8,128)(2,1)S(1)} %copy.4), channel_id=1, replica_groups=mesh['loop'=64,'grp'=4] {'grp'}, dimensions={1}, use_global_device_ids=true | all-gather | bytes 552960 | tf_op jit(solution)/shard_map/all_gather | solution.py:41
  23.5 5.1 copy-done
  28.7 432.8 %while.19 = (s32[]{:T(128)}, bf16[2,48,1152]{2,1,0:T(8,128)(2,1)S(1)}, f32[64,48,1152]{2,1,0:T(8,128)}, f32[192,1152]{1,0:T(8,128)S(1)}, s32[]{:T(128)}, /*index...) while((s32[]{:T(128)}, bf16[2,48,1152]{2,1,0:T(8,128)(2,1)S(1)}, ...), condition=%wide.region_3.4_spmd, body=%wide.region_2.3_spmd.sunk | while | flops 127862800 | bytes 6746611 | solution.py:90
  30.8 3.3 collective-permute-done
  38.5 7.6 collective-permute-start
  48.5 6.3 collective-permute-done.1
  61.2 2.7 collective-permute-done
  63.9 4.5 collective-permute-done.1
  74.8 2.7 collective-permute-done
  77.5 4.3 collective-permute-done.1
  88.2 2.7 collective-permute-done
  90.9 4.3 collective-permute-done.1
  104.3 4.3 collective-permute-done.1
  115.1 2.7 collective-permute-done
  117.8 4.3 collective-permute-done.1
  128.5 2.7 collective-permute-done
  131.2 4.3 collective-permute-done.1
  141.9 2.7 collective-permute-done
  144.6 4.3 collective-permute-done.1
  155.3 2.7 collective-permute-done
  158.0 4.3 collective-permute-done.1
  168.8 3.6 collective-permute-done
  172.4 4.2 collective-permute-done.1
  183.2 2.8 collective-permute-done
  186.0 4.3 collective-permute-done.1
  196.7 2.7 collective-permute-done
  199.5 4.3 collective-permute-done.1
  210.2 2.7 collective-permute-done
  212.9 4.4 collective-permute-done.1
  223.7 2.7 collective-permute-done
  226.4 4.3 collective-permute-done.1
  239.8 4.3 collective-permute-done.1
  250.6 2.7 collective-permute-done
  253.3 4.2 collective-permute-done.1
  264.0 2.7 collective-permute-done
  266.7 4.3 collective-permute-done.1
  277.3 2.7 collective-permute-done
  280.1 4.3 collective-permute-done.1
  290.7 2.7 collective-permute-done
  293.5 4.3 collective-permute-done.1
  306.9 4.3 collective-permute-done.1
  317.6 3.5 collective-permute-done
  321.2 4.4 collective-permute-done.1
  332.1 2.9 collective-permute-done
  335.1 4.3 collective-permute-done.1
  345.8 2.7 collective-permute-done
  348.5 4.2 collective-permute-done.1
  359.1 2.7 collective-permute-done
  361.9 4.4 collective-permute-done.1
  375.4 4.3 collective-permute-done.1
  388.8 4.4 collective-permute-done.1
  402.2 4.3 collective-permute-done.1
  413.0 2.7 collective-permute-done
  415.7 4.8 collective-permute-done.1
  426.9 2.7 collective-permute-done
  429.6 3.7 collective-permute-done.1
  439.7 10.7 %collective-permute-done = bf16[1,48,1152]{2,1,0:T(8,128)(2,1)S(1)} collective-permute-done((bf16[1,48,1152]{2,1,0:T(8,128)(2,1)S(1)}, bf16[1,48,1152]{2,1,0:T(8,128)(2,1)S(1)}, u32[]{:S(2)}, u32[]{:S(2)}) %collective-permute-start) | collective-permute-done | bytes 110624 | tf_op jit(solution)/shard_map/while/body/eval_jaxpr/ppermute | solution.py:19
  450.4 6.8 collective-permute-done.1
  461.6 6.9 collective-permute-done.2
  470.6 23.5 %all-to-all-start = ((f32[64,48,1152]{2,1,0:T(8,128)}), f32[64,48,1152]{2,1,0:T(8,128)}, u32[]{:S(2)}, u32[]{:S(2)}) async-start(f32[64,48,1152]{2,1,0:T(8,128)} %fusion.12), calls=%async_computation | async-start | bytes 28311552 | tf_op jit(solution)/shard_map/all_to_all | solution.py:96
  496.0 49.0 %reduce-scatter.4.cloned.1.call-done = f32[288,192]{1,0:T(8,128)} async-done(((f32[1152,192]{1,0:T(8,128)}), f32[288,192]{1,0:T(8,128)}) %reduce-scatter.4.cloned.1.call-update) | async-done | bytes 221200
  546.3 8.0 %psum.7 = f32[192]{0:T(256)S(1)} all-reduce(f32[192]{0:T(256)S(1)} %multiply_reduce_fusion), channel_id=1, replica_groups=mesh['loop'=64,'grp'=4] {'grp'}, use_global_device_ids=true, to_apply=%region_6.7 | all-reduce | flops 192 | bytes 1536 | tf_op jit(solution)/shard_map/psum | solution.py:102
  555.1 196.5 %all-to-all-done = f32[64,48,1152]{2,1,0:T(8,128)} async-done(((f32[64,48,1152]{2,1,0:T(8,128)}), f32[64,48,1152]{2,1,0:T(8,128)}, u32[]{:S(2)}, u32[]{:S(2)}) %all-to-all-start) | async-done | bytes 14155808 | tf_op jit(solution)/shard_map/all_to_all | solution.py:96
  751.6 5.7 reduce_sum.48
  (349 shorter events, 228.7 us)
Async XLA Ops:
  28.7 5.4 collective-permute-start
  29.2 5.0 collective-permute-start.1
  38.5 9.9 %collective-permute-start = (bf16[1,48,1152]{2,1,0:T(8,128)(2,1)S(1)}, bf16[1,48,1152]{2,1,0:T(8,128)(2,1)S(1)}, u32[]{:S(2)}, u32[]{:S(2)}) collective-permute-start(bf16[1,48,1152]{2,1,0:T(8,128)(2,1)S(1)} %get-tuple-element.221), channel_id=1, source_target_pairs={{4,0},{8,4},{12,8},{16,12},{20,16},{24,20},{28,24},{32,28},{36,32}... | collective-permute-start | bytes 331784 | tf_op jit(solution)/shard_map/while/body/eval_jaxpr/ppermute | solution.py:19
  46.1 8.7 %collective-permute-start.1 = (bf16[1,48,1152]{2,1,0:T(8,128)(2,1)S(1)}, bf16[1,48,1152]{2,1,0:T(8,128)(2,1)S(1)}, u32[]{:S(2)}, u32[]{:S(2)}) collective-permute-start(bf16[1,48,1152]{2,1,0:T(8,128)(2,1)S(1)} %get-tuple-element.222), channel_id=1, source_target_pairs={{0,4},{4,8},{8,12},{12,16},{16,20},{20,24},{24,28},{28,32},{32,36}... | collective-permute-start | bytes 331784 | tf_op jit(solution)/shard_map/while/body/eval_jaxpr/ppermute | solution.py:16
  59.1 4.8 collective-permute-start
  61.2 7.2 collective-permute-start.1
  72.7 4.8 collective-permute-start
  74.8 7.0 collective-permute-start.1
  86.1 4.8 collective-permute-start
  88.2 7.0 collective-permute-start.1
  99.5 4.8 collective-permute-start
  101.6 7.1 collective-permute-start.1
  113.0 4.8 collective-permute-start
  115.1 7.0 collective-permute-start.1
  126.4 4.8 collective-permute-start
  128.5 7.0 collective-permute-start.1
  139.7 4.8 collective-permute-start
  141.9 7.0 collective-permute-start.1
  153.2 4.8 collective-permute-start
  155.3 7.0 collective-permute-start.1
  166.6 5.8 collective-permute-start
  168.8 7.8 %collective-permute-start.1 = (bf16[1,48,1152]{2,1,0:T(8,128)(2,1)S(1)}, bf16[1,48,1152]{2,1,0:T(8,128)(2,1)S(1)}, u32[]{:S(2)}, u32[]{:S(2)}) collective-permute-start(bf16[1,48,1152]{2,1,0:T(8,128)(2,1)S(1)} %get-tuple-element.222), channel_id=1, source_target_pairs={{0,4},{4,8},{8,12},{12,16},{16,20},{20,24},{24,28},{28,32},{32,36}... | collective-permute-start | bytes 331784 | tf_op jit(solution)/shard_map/while/body/eval_jaxpr/ppermute | solution.py:16
  180.9 5.2 collective-permute-start
  183.2 7.2 collective-permute-start.1
  194.6 4.8 collective-permute-start
  196.5 7.3 collective-permute-start.1
  208.1 4.8 collective-permute-start
  210.2 7.2 collective-permute-start.1
  221.6 4.8 collective-permute-start
  223.7 7.1 collective-permute-start.1
  235.0 4.8 collective-permute-start
  237.1 7.0 collective-permute-start.1
  248.5 4.8 collective-permute-start
  250.6 7.0 collective-permute-start.1
  261.9 4.8 collective-permute-start
  263.9 7.0 collective-permute-start.1
  275.2 4.8 collective-permute-start
  277.3 7.1 collective-permute-start.1
  288.6 4.8 collective-permute-start
  290.7 7.0 collective-permute-start.1
  302.0 4.8 collective-permute-start
  304.1 7.1 collective-permute-start.1
  315.5 5.7 collective-permute-start
  317.6 8.0 %collective-permute-start.1 = (bf16[1,48,1152]{2,1,0:T(8,128)(2,1)S(1)}, bf16[1,48,1152]{2,1,0:T(8,128)(2,1)S(1)}, u32[]{:S(2)}, u32[]{:S(2)}) collective-permute-start(bf16[1,48,1152]{2,1,0:T(8,128)(2,1)S(1)} %get-tuple-element.222), channel_id=1, source_target_pairs={{0,4},{4,8},{8,12},{12,16},{16,20},{20,24},{24,28},{28,32},{32,36}... | collective-permute-start | bytes 331784 | tf_op jit(solution)/shard_map/while/body/eval_jaxpr/ppermute | solution.py:16
  329.9 5.1 collective-permute-start
  332.1 7.2 collective-permute-start.1
  343.7 4.8 collective-permute-start
  345.5 7.3 collective-permute-start.1
  357.0 4.8 collective-permute-start
  359.1 7.2 collective-permute-start.1
  370.5 4.8 collective-permute-start
  372.7 7.0 collective-permute-start.1
  383.9 4.8 collective-permute-start
  386.1 7.1 collective-permute-start.1
  399.5 7.0 collective-permute-start.1
  410.9 4.8 collective-permute-start
  412.9 7.6 collective-permute-start.1
  424.8 4.8 collective-permute-start
  426.3 7.0 collective-permute-start.1
  437.6 12.8 %collective-permute-start = (bf16[1,48,1152]{2,1,0:T(8,128)(2,1)S(1)}, bf16[1,48,1152]{2,1,0:T(8,128)(2,1)S(1)}, u32[]{:S(2)}, u32[]{:S(2)}) collective-permute-start(bf16[1,48,1152]{2,1,0:T(8,128)(2,1)S(1)} %get-tuple-element.221), channel_id=1, source_target_pairs={{4,0},{8,4},{12,8},{16,12},{20,16},{24,20},{28,24},{32,28},{36,32}... | collective-permute-start | bytes 331784 | tf_op jit(solution)/shard_map/while/body/eval_jaxpr/ppermute | solution.py:19
  439.7 17.4 %collective-permute-start.1 = (bf16[1,48,1152]{2,1,0:T(8,128)(2,1)S(1)}, bf16[1,48,1152]{2,1,0:T(8,128)(2,1)S(1)}, u32[]{:S(2)}, u32[]{:S(2)}) collective-permute-start(bf16[1,48,1152]{2,1,0:T(8,128)(2,1)S(1)} %get-tuple-element.222), channel_id=1, source_target_pairs={{0,4},{4,8},{8,12},{12,16},{16,20},{20,24},{24,28},{28,32},{32,36}... | collective-permute-start | bytes 331784 | tf_op jit(solution)/shard_map/while/body/eval_jaxpr/ppermute | solution.py:16
  461.4 7.0 collective-permute-start.2
  470.6 281.0 %all-to-all-start = ((f32[64,48,1152]{2,1,0:T(8,128)}), f32[64,48,1152]{2,1,0:T(8,128)}, u32[]{:S(2)}, u32[]{:S(2)}) async-start(f32[64,48,1152]{2,1,0:T(8,128)} %fusion.12), calls=%async_computation | async-start | bytes 28311552 | tf_op jit(solution)/shard_map/all_to_all | solution.py:96
  494.2 50.8 %reduce-scatter.4.cloned.1.call-start = ((), (), s32[]{:S(2)}) async-start(), calls=%async_computation.2 | async-start | bytes 1474560
  (4 other events, 348.6 us)
Sparse Core Ops, SparseCore 0:
  497.8 47.1 reduce-scatter.3
where the time goes:
time: 767 us; the launch traced here: 765 us
  waiting for transfers between devices  481 us (63%)
  other arithmetic  113 us (15%)
  starting transfers between devices  95 us (12%)
  matrix products  33.1 us (4%)
  blocking collectives  17 us (2%)
  between operations  14.2 us (2%)
  local copies, waits for them, and re-layouts  11.2 us (1%)
    all_to_all x1, waiting for transfers between devices, on_device(): lax.all_to_all(grad_store, 'loop', split_axis=0, concat_axis=0, tiled=True)  197 us
    ppermute x32, waiting for transfers between devices, padded_2(): lax.ppermute(lax.slice_in_dim(block, block.shape[dim] - width, None, axis...  141 us
    dynamic_update_slice x62, other arithmetic, deposit(): return lax.dynamic_update_slice(grad_store, previous + piece[None], corner)  103 us
    ppermute x31, waiting for transfers between devices, padded_2(): lax.ppermute(lax.slice_in_dim(block, 0, width, axis=dim), axis, backward)  94.4 us
    ppermute x31, starting transfers between devices, padded_2(): lax.ppermute(lax.slice_in_dim(block, 0, width, axis=dim), axis, backward)  68.4 us
    unnamed x2, waiting for transfers between devices  49.1 us
    all_to_all x1, starting transfers between devices, on_device(): lax.all_to_all(grad_store, 'loop', split_axis=0, concat_axis=0, tiled=True)  23.5 us
  transfers between devices with their start and end apart: 65, of which 65 were waited for; matrix products, arithmetic and copies ran while one was open for 1% of the time, Pallas kernels for 0%

commit v1 on v0

v1 whole, which is shorter than its diff:
```python
import jax
import jax.numpy as jnp
from jax import lax
from jax.experimental import pallas as pl
from jax.experimental.pallas import tpu as pltpu
from jax.sharding import PartitionSpec as P

LOGIT_SCALE = 16.0
LOGIT_BIAS = -4.0
BF16 = jnp.bfloat16
F32 = jnp.float32
R = 48
D = 1152
Q = 288
N = 768
PIECES = 3
PR = R // PIECES
COPIES = 256
MESH = pl.DeviceIdType.MESH
VIA_P = (0, 2)


def neighbours():
    loop = lax.axis_index("loop")
    grp = lax.axis_index("grp")
    z = loop // 8
    x = (grp // 2) * 2 + (loop // 4) % 2
    y = loop % 4
    c = grp % 2

    def dev(dz, dx, dy, flip=0):
        zz = (z + dz + 8) % 8
        xx = (x + dx + 4) % 4
        yy = (y + dy + 4) % 4
        return (zz * 8 + (xx % 2) * 4 + yy, (xx // 2) * 2 + (c + flip) % 2)

    f = 1 - 2 * c
    return {
        "zp": dev(f, 0, 0),
        "zm": dev(-f, 0, 0),
        "ap": dev(0, 1 - c, c),
        "am": dev(0, c - 1, -c),
        "bp": dev(0, c, 1 - c),
        "bm": dev(0, -c, c - 1),
        "sib": dev(0, 0, 0, 1),
        "g1": (loop, (grp + 1) % 4),
        "g2": (loop, (grp + 2) % 4),
        "g3": (loop, (grp + 3) % 4),
    }, loop, grp


def unit_of(values):
    scale = lax.rsqrt(jnp.sum(values * values, axis=-1, keepdims=True) + 1e-06)
    return values * scale, scale


def kernel(
    img, txt, oimg, otxt,
    xin, tin, ibuf, tbuf, coef, ip, tp, iscale, iunit,
    sib_out, sib_in, z_out, z_in, b_out, b_in, a_out, a_in, g_out, g_in,
    send_sems, recv_sems, local_sems,
):
    dev, loop, grp = neighbours()
    copies = {}

    def send(key, src, dst, to):
        index = len(copies)
        copy = pltpu.make_async_remote_copy(
            src_ref=src, dst_ref=dst, send_sem=send_sems.at[index],
            recv_sem=recv_sems.at[index], device_id=dev[to], device_id_type=MESH,
        )
        copy.start()
        copies[key] = copy

    def got(key):
        copies[key].wait_recv()

    own_rows = pl.ds(pl.multiple_of(grp * R, 16), R)
    load_t = pltpu.make_async_copy(txt, tin, local_sems.at[0])
    load_t.start()
    load_i = pltpu.make_async_copy(img.at[own_rows, :], xin.at[grp], local_sems.at[1])
    load_i.start()

    barrier = pltpu.get_barrier_semaphore()
    greeted = ("zp", "zm", "ap", "am", "bp", "bm", "g1", "g2", "g3")
    for name in greeted:
        pl.semaphore_signal(barrier, inc=1, device_id=dev[name], device_id_type=MESH)
    pl.semaphore_wait(barrier, len(greeted))

    for step in (1, 2, 3):
        there = (grp + step) % 4
        rows = pl.ds(pl.multiple_of(there * R, 16), R)
        send(("x", step), img.at[rows, :], xin.at[grp], "g%d" % step)

    pieces = range(PIECES)

    def rows_of(slot, piece):
        return pl.ds(slot * R + piece * PR, PR)

    load_t.wait()
    unit, tscale = unit_of(tin[...].astype(F32))
    tbuf[pl.ds(0, R), :] = unit.astype(BF16)

    def send_t(to, slot, new, piece):
        send(("t", new, piece), tbuf.at[rows_of(slot, piece), :], tbuf.at[rows_of(new, piece), :], to)

    def send_s(slot, piece):
        send(("s", slot, piece), tbuf.at[rows_of(slot, piece), :], tbuf.at[rows_of(slot + 8, piece), :], "sib")

    def send_i(to, slot, new, piece):
        send(("i", new, piece), ibuf.at[rows_of(slot, piece), :], ibuf.at[rows_of(new, piece), :], to)

    for p in pieces:
        send_t("zm", 0, 1, p)
        send_t("zp", 0, 7, p)
    for p in pieces:
        send_s(0, p)

    load_i.wait()
    for step in (1, 2, 3):
        got(("x", step))
    values = jnp.concatenate([xin[j].astype(F32) for j in range(4)], axis=1)
    unit_i, scale_i = unit_of(values)
    iscale[...] = jnp.broadcast_to(scale_i, (R, 128))
    iunit[...] = unit_i
    ibuf[pl.ds(0, R), :] = unit_i.astype(BF16)

    for p in pieces:
        send_i("am", 0, 1, p)
        send_i("ap", 0, 3, p)
    for p in pieces:
        send_i("bm", 0, 4, p)
        send_i("bp", 0, 12, p)

    def ring_t(new_m, new_p):
        for p in pieces:
            got(("t", new_m, p))
            if new_m < 4:
                send_t("zm", new_m, new_m + 1, p)
            if new_p is not None:
                got(("t", new_p, p))
                if new_p > 5:
                    send_t("zp", new_p, new_p - 1, p)
        for p in pieces:
            send_s(new_m, p)
            if new_p is not None:
                send_s(new_p, p)

    def far_b(d1):
        for p in pieces:
            if d1 in VIA_P:
                got(("i", 4 + d1, p))
                send_i("bm", 4 + d1, 8 + d1, p)
            else:
                got(("i", 12 + d1, p))
                send_i("bp", 12 + d1, 8 + d1, p)

    def near_b(d1):
        for p in pieces:
            got(("i", d1, p))
            send_i("bm", d1, 4 + d1, p)
            send_i("bp", d1, 12 + d1, p)

    ring_t(1, 7)
    for p in pieces:
        got(("i", 1, p))
        send_i("am", 1, 2, p)
        send_i("bm", 1, 5, p)
        send_i("bp", 1, 13, p)
    near_b(3)
    far_b(0)
    ring_t(2, 6)
    near_b(2)
    far_b(1)
    far_b(3)
    ring_t(3, 5)
    far_b(2)
    ring_t(4, None)
    for p in pieces:
        for slot in range(8):
            got(("s", slot, p))
        for d1 in range(4):
            got(("i", 8 + d1, p))
            if d1 in VIA_P:
                got(("i", 12 + d1, p))
            else:
                got(("i", 4 + d1, p))

    def one_tile(m, carry):
        rows = pl.ds(pl.multiple_of(m * 256, 256), 256)
        logits = LOGIT_SCALE * lax.dot_general(
            ibuf[rows, :], tbuf[...], (((1,), (1,)), ((), ())), preferred_element_type=F32
        ) + LOGIT_BIAS
        row_ids = m * 256 + lax.broadcasted_iota(jnp.int32, (256, N), 0)
        col_ids = lax.broadcasted_iota(jnp.int32, (256, N), 1)
        labels = jnp.where((row_ids == col_ids) & (row_ids < R), 1.0, 0.0)
        tile = (LOGIT_SCALE * (jax.nn.sigmoid(logits) - labels)).astype(BF16)
        coef[rows, :] = tile
        ip[rows, :] = jnp.dot(tile, tbuf[...], preferred_element_type=F32)
        return carry

    lax.fori_loop(0, 3, one_tile, 0)
    for n in range(3):
        cols = pl.ds(n * 256, 256)
        tp[cols, :] = lax.dot_general(
            coef[:, cols], ibuf[...], (((0,), (0,)), ((), ())), preferred_element_type=F32
        )

    for k in (4, 5, 3, 6, 2, 7, 1, 0):
        sib_out[pl.ds(k * R, R), :] = tp[pl.ds((8 + k) * R, R), :].astype(BF16)
        for p in pieces:
            rows = rows_of(k, p)
            send(("so", k, p), sib_out.at[rows, :], sib_in.at[rows, :], "sib")

    def send_b(to, slot, new, piece):
        rows = rows_of(slot, piece)
        send(("bo", slot, piece), b_out.at[rows, :], b_in.at[rows_of(new, piece), :], to)

    def b_first(d1):
        for p in pieces:
            rows = rows_of(8 + d1, p)
            b_out[rows, :] = ip[rows, :].astype(BF16)
            if d1 in VIA_P:
                send_b("bp", 8 + d1, 4 + d1, p)
            else:
                send_b("bm", 8 + d1, 12 + d1, p)

    def b_direct(d1):
        for p in pieces:
            slot = 12 + d1 if d1 in VIA_P else 4 + d1
            rows = rows_of(slot, p)
            b_out[rows, :] = ip[rows, :].astype(BF16)
            if d1 in VIA_P:
                send_b("bm", slot, d1, p)
            else:
                send_b("bp", slot, 8 + d1, p)

    def b_second(d1):
        for p in pieces:
            slot = 4 + d1 if d1 in VIA_P else 12 + d1
            rows = rows_of(slot, p)
            got(("bo", 8 + d1, p))
            b_out[rows, :] = (ip[rows, :] + b_in[rows, :].astype(F32)).astype(BF16)
            if d1 in VIA_P:
                send_b("bp", slot, 8 + d1, p)
            else:
                send_b("bm", slot, d1, p)

    def b_sum(d1, p):
        got(("bo", 4 + d1, p))
        got(("bo", 12 + d1, p))
        near = rows_of(d1, p)
        far = rows_of(8 + d1, p)
        return ip[near, :] + b_in[near, :].astype(F32) + b_in[far, :].astype(F32)

    def z_first(k, to, new):
        for p in pieces:
            rows = rows_of(k, p)
            got(("so", k, p))
            total = tp[rows, :] + sib_in[rows, :].astype(F32)
            if k not in (4, 5):
                got(("zo", k + 1 if k < 4 else k - 1, p))
                total = total + z_in[rows, :].astype(F32)
            z_out[rows, :] = total.astype(BF16)
            send(("zo", k, p), z_out.at[rows, :], z_in.at[rows_of(new, p), :], to)

    for d1 in (2, 1, 3, 0):
        b_first(d1)
    z_first(4, "zp", 3)
    z_first(5, "zm", 6)
    for d1 in (2, 1, 3, 0):
        b_direct(d1)
    z_first(3, "zp", 2)
    for d1 in (2, 1):
        b_second(d1)
    z_first(6, "zm", 7)
    for d1 in (3, 0):
        b_second(d1)
    z_first(2, "zp", 1)

    def send_a(to, slot, new, total, p):
        rows = rows_of(slot, p)
        a_out[rows, :] = total.astype(BF16)
        send(("ao", slot, p), a_out.at[rows, :], a_in.at[rows_of(new, p), :], to)

    for p in pieces:
        send_a("ap", 2, 1, b_sum(2, p), p)
    z_first(7, "zm", 4)
    for p in pieces:
        send_a("am", 3, 0, b_sum(3, p), p)
    z_first(1, "zp", 0)
    for p in pieces:
        total = b_sum(1, p)
        got(("ao", 2, p))
        send_a("ap", 1, 2, total + a_in[rows_of(1, p), :].astype(F32), p)
    for p in pieces:
        total = b_sum(0, p)
        got(("ao", 3, p))
        total = total + a_in[rows_of(0, p), :].astype(F32)
        got(("ao", 1, p))
        total = total + a_in[rows_of(2, p), :].astype(F32)
        ip[rows_of(0, p), :] = total

    def back_norm(unit_rows, scale, direction):
        inner = jnp.sum(unit_rows * direction, axis=-1, keepdims=True)
        return scale * (direction - unit_rows * inner)

    image_grad = back_norm(iunit[...], iscale[:, :1], ip[pl.ds(0, R), :])
    for j in range(4):
        g_out[j] = image_grad[:, j * Q:(j + 1) * Q].astype(BF16)
    for step in (1, 2, 3):
        send(("g", step), g_out.at[(grp + step) % 4], g_in.at[grp], "g%d" % step)
    keep = pltpu.make_async_copy(g_out.at[grp], g_in.at[grp], local_sems.at[2])
    keep.start()

    for p in pieces:
        got(("so", 0, p))
        got(("zo", 1, p))
        got(("zo", 7, p))
    own = pl.ds(0, R)
    direction = tp[own, :] + sib_in[own, :].astype(F32)
    direction = direction + z_in[own, :].astype(F32) + z_in[pl.ds(4 * R, R), :].astype(F32)
    text_unit, text_scale = unit_of(tin[...].astype(F32))
    otxt[...] = back_norm(text_unit, text_scale, direction).astype(BF16)

    keep.wait()
    for step in (1, 2, 3):
        got(("g", step))
    for j in range(4):
        oimg[pl.ds(j * R, R), :] = g_in[j]
    for copy in copies.values():
        copy.wait_send()


def on_device(image_features, text_features):
    vmem = pltpu.VMEM
    return pl.pallas_call(
        kernel,
        out_shape=(
            jax.ShapeDtypeStruct((4 * R, Q), BF16),
            jax.ShapeDtypeStruct((R, D), BF16),
        ),
        in_specs=[pl.BlockSpec(memory_space=pl.ANY)] * 2,
        out_specs=(pl.BlockSpec(memory_space=vmem), pl.BlockSpec(memory_space=vmem)),
        scratch_shapes=[
            vmem((4, R, Q), BF16),
            vmem((R, D), BF16),
            vmem((N, D), BF16),
            vmem((N, D), BF16),
            vmem((N, N), BF16),
            vmem((N, D), F32),
            vmem((N, D), F32),
            vmem((R, 128), F32),
            vmem((R, D), F32),
            vmem((8 * R, D), BF16),
            vmem((8 * R, D), BF16),
            vmem((8 * R, D), BF16),
            vmem((8 * R, D), BF16),
            vmem((N, D), BF16),
            vmem((N, D), BF16),
            vmem((4 * R, D), BF16),
            vmem((4 * R, D), BF16),
            vmem((4, R, Q), BF16),
            vmem((4, R, Q), BF16),
            pltpu.SemaphoreType.DMA((COPIES,)),
            pltpu.SemaphoreType.DMA((COPIES,)),
            pltpu.SemaphoreType.DMA((4,)),
        ],
        compiler_params=pltpu.CompilerParams(
            collective_id=0, has_side_effects=True, vmem_limit_bytes=50 * 1024 * 1024
        ),
        cost_estimate=pl.CostEstimate(
            flops=6 * N * N * D, bytes_accessed=8 * R * D, transcendentals=N * N
        ),
    )(image_features, text_features)


def solution(mesh):
    placed = (P("loop", "grp"), P(("loop", "grp"), None))
    return jax.shard_map(
        on_device, mesh=mesh, in_specs=placed, out_specs=placed, check_vma=False
    )
```

time: 767 us -> 65.2 us (0.09)
  the two profiles are of different devices: /device:TPU:16 before, /device:TPU:1 now
where the time goes in v1:
time: 65.2 us; the launch traced here: 65.1 us
  Pallas kernels  61.3 us (94%)
  local copies, waits for them, and re-layouts  3.11 us (5%)
    pallas_call x1, Pallas kernels, on_device(): pl.pallas_call(kernel, out_shape=(jax.ShapeDtypeStruct((4 * R, Q), BF16),...  61.3 us
    unnamed x6, local copies, waits for them, and re-layouts  3.11 us

profile of v1, /device:TPU:1, one launch (start us, length us, event | category | flops | bytes accessed | tf_op | source)
XLA Modules:
  0.0 65.1 jit_solution(362658201176381792)
XLA Ops:
  0.6 0.0 copy-start
  0.6 0.9 %copy-done = bf16[192,288]{1,0:T(8,128)(2,1)S(1)} copy-done((bf16[192,288]{1,0:T(8,128)(2,1)S(1)}, bf16[192,288]{1,0:T(8,128)(2,1)}, u32[]{:S(2)}) %copy-start) | copy-done | bytes 110616
  1.5 0.0 copy-start.1
  1.5 0.9 %copy-done.1 = bf16[48,1152]{1,0:T(8,128)(2,1)S(1)} copy-done((bf16[48,1152]{1,0:T(8,128)(2,1)S(1)}, bf16[48,1152]{1,0:T(8,128)(2,1)}, u32[]{:S(2)}) %copy-start.1) | copy-done | bytes 110616
  2.4 61.3 %shard_map.41 = (bf16[192,288]{1,0:T(8,128)(2,1)S(1)}, bf16[48,1152]{1,0:T(8,128)(2,1)S(1)}) custom-call(bf16[192,288]{1,0:T(8,128)(2,1)S(1)} %copy-done, bf16[48,1152]{1,0:T(8,128)(2,1)S(1)} %copy-done.1), custom_call_target="tpu_custom_call" | custom-call | flops 4076863488 | bytes 442368 | tf_op jit(solution)/shard_map/pallas_call | solution.py:337
  63.8 0.7 %copy.6 = bf16[192,288]{1,0:T(8,128)(2,1)} copy(bf16[192,288]{1,0:T(8,128)(2,1)S(1)} %get-tuple-element.4) | data formatting | bytes 221184
  64.4 0.6 copy.7
Async XLA Ops:
  0.6 0.9 %copy-start = (bf16[192,288]{1,0:T(8,128)(2,1)S(1)}, bf16[192,288]{1,0:T(8,128)(2,1)}, u32[]{:S(2)}) copy-start(bf16[192,288]{1,0:T(8,128)(2,1)} %img.1) | copy-start | bytes 331780
  1.5 0.9 %copy-start.1 = (bf16[48,1152]{1,0:T(8,128)(2,1)S(1)}, bf16[48,1152]{1,0:T(8,128)(2,1)}, u32[]{:S(2)}) copy-start(bf16[48,1152]{1,0:T(8,128)(2,1)} %txt.1) | copy-start | bytes 331780

commit v2 on v1

v2 whole, which is shorter than its diff:
```python
import jax
import jax.numpy as jnp
from jax import lax
from jax.experimental import pallas as pl
from jax.experimental.pallas import tpu as pltpu
from jax.sharding import PartitionSpec as P

LOGIT_SCALE = 16.0
LOGIT_BIAS = -4.0
BF16 = jnp.bfloat16
F32 = jnp.float32
R = 48
D = 1152
Q = 288
N = 768
PIECES = 3
PR = R // PIECES
SENDS = 9
RECVS = 70
GREETED = ("zp", "zm", "ap", "am", "bp", "bm", "y2", "g1", "g2", "g3")
MESH = pl.DeviceIdType.MESH
VIA_P = (0, 2)


def neighbours():
    loop = lax.axis_index("loop")
    grp = lax.axis_index("grp")
    z = loop // 8
    x = (grp // 2) * 2 + (loop // 4) % 2
    y = loop % 4
    c = grp % 2

    def dev(dz, dx, dy, flip=0):
        zz = (z + dz + 8) % 8
        xx = (x + dx + 4) % 4
        yy = (y + dy + 4) % 4
        return (zz * 8 + (xx % 2) * 4 + yy, (xx // 2) * 2 + (c + flip) % 2)

    f = 1 - 2 * c
    return {
        "zp": dev(f, 0, 0),
        "zm": dev(-f, 0, 0),
        "ap": dev(0, 1 - c, c),
        "am": dev(0, c - 1, -c),
        "bp": dev(0, c, 1 - c),
        "bm": dev(0, -c, c - 1),
        "a2": dev(0, 2 - 2 * c, 2 * c),
        "b2": dev(0, 2 * c, 2 - 2 * c),
        "y2": dev(0, 0, 2),
        "sib": dev(0, 0, 0, 1),
        "g1": (loop, (grp + 1) % 4),
        "g2": (loop, (grp + 2) % 4),
        "g3": (loop, (grp + 3) % 4),
    }, loop, grp


def unit_of(values):
    scale = lax.rsqrt(jnp.sum(values * values, axis=-1, keepdims=True) + 1e-06)
    return values * scale, scale


def kernel(
    img, txt, oimg, otxt,
    xin, tin, ibuf, tbuf, coef, ip, tp, iscale, iunit,
    sib_out, sib_in, z_out, z_in, b_out, b_in, a_out, a_in, g_out, g_in,
    send_sems, recv_sems, local_sems,
):
    dev, loop, grp = neighbours()
    send_ids = {}
    recv_ids = {}

    def copy_of(kind, key, src, dst, to):
        out = send_ids.setdefault(kind, len(send_ids))
        arrive = recv_ids.setdefault(key, len(recv_ids))
        return pltpu.make_async_remote_copy(
            src_ref=src, dst_ref=dst, send_sem=send_sems.at[out],
            recv_sem=recv_sems.at[arrive], device_id=dev[to], device_id_type=MESH,
        )

    def got(key, ref):
        pltpu.make_async_copy(ref, ref, recv_sems.at[recv_ids[key]]).wait()

    def left(kind, ref):
        pltpu.make_async_copy(ref, ref, send_sems.at[send_ids[kind]]).wait()

    def blocks(slot, count=1):
        return pl.ds(slot * R, count * R)

    def rows_of(slot, piece):
        return pl.ds(slot * R + piece * PR, PR)

    pieces = range(PIECES)
    own_rows = pl.ds(pl.multiple_of(grp * R, 16), R)
    load_t = pltpu.make_async_copy(txt, tin, local_sems.at[0])
    load_t.start()
    load_i = pltpu.make_async_copy(img.at[own_rows, :], xin.at[grp], local_sems.at[1])
    load_i.start()

    barrier = pltpu.get_barrier_semaphore()
    for name in GREETED:
        pl.semaphore_signal(barrier, inc=1, device_id=dev[name], device_id_type=MESH)
    load_t.wait()
    unit, tscale = unit_of(tin[...].astype(F32))
    tbuf[blocks(0), :] = unit.astype(BF16)
    load_i.wait()
    pl.semaphore_wait(barrier, len(GREETED))

    for step in (1, 2, 3):
        there = (grp + step) % 4
        rows = pl.ds(pl.multiple_of(there * R, 16), R)
        copy_of("x", "x", img.at[rows, :], xin.at[grp], "g%d" % step).start()

    def send_t(to, slot, new, piece):
        key = ("t", new) if new in (4, 5) else ("t", new, piece)
        copy_of("t", key, tbuf.at[rows_of(slot, piece), :], tbuf.at[rows_of(new, piece), :], to).start()

    def send_s(slot):
        copy_of("s", "s", tbuf.at[blocks(slot), :], tbuf.at[blocks(slot + 8), :], "sib").start()

    for p in pieces:
        send_t("zm", 0, 1, p)
        send_t("zp", 0, 7, p)
    send_s(0)

    got("x", xin.at[pl.ds(0, 3)])
    values = jnp.concatenate([xin[j].astype(F32) for j in range(4)], axis=1)
    unit_i, scale_i = unit_of(values)
    ibuf[blocks(0), :] = unit_i.astype(BF16)

    def send_i(to, slot, new):
        copy_of("i", ("i", new), ibuf.at[blocks(slot), :], ibuf.at[blocks(new), :], to).start()

    def send_ip(to, slot, new, piece):
        copy_of(
            "i", ("i", new, piece), ibuf.at[rows_of(slot, piece), :], ibuf.at[rows_of(new, piece), :], to
        ).start()

    def send_far(to, slot, new, piece):
        copy_of(
            "i", "far", ibuf.at[rows_of(slot, piece), :], ibuf.at[rows_of(new, piece), :], to
        ).start()

    def near_b(d1):
        if d1 in VIA_P:
            for p in pieces:
                send_ip("bm", d1, 4 + d1, p)
            send_i("bp", d1, 12 + d1)
        else:
            for p in pieces:
                send_ip("bp", d1, 12 + d1, p)
            send_i("bm", d1, 4 + d1)

    def far_b(d1):
        for p in pieces:
            slot = 4 + d1 if d1 in VIA_P else 12 + d1
            got(("i", slot, p), ibuf.at[rows_of(slot, p), :])
            send_far("bm" if d1 in VIA_P else "bp", slot, 8 + d1, p)

    send_i("am", 0, 1)
    send_i("ap", 0, 3)
    send_i("a2", 0, 2)
    near_b(0)
    iscale[...] = jnp.broadcast_to(scale_i, (R, 128))
    iunit[...] = unit_i

    def ring_t(new_m, new_p):
        for p in pieces:
            got(("t", new_m, p), tbuf.at[rows_of(new_m, p), :])
            send_t("zm", new_m, new_m + 1, p)
            if new_p > 5:
                got(("t", new_p, p), tbuf.at[rows_of(new_p, p), :])
                send_t("zp", new_p, new_p - 1, p)
        send_s(new_m)
        if new_p == 5:
            got(("t", 5), tbuf.at[blocks(5), :])
        send_s(new_p)

    ring_t(1, 7)
    ring_t(2, 6)
    for d1 in (1, 3):
        got(("i", d1), ibuf.at[blocks(d1), :])
        near_b(d1)
    far_b(0)
    got(("i", 2), ibuf.at[blocks(2), :])
    near_b(2)
    ring_t(3, 5)
    far_b(1)
    far_b(3)
    got(("t", 4), tbuf.at[blocks(4), :])
    send_s(4)
    far_b(2)
    got("s", tbuf.at[blocks(8, 8), :])

    def coef_of(slot, count):
        rows = blocks(slot, count)
        logits = LOGIT_SCALE * lax.dot_general(
            ibuf[rows, :], tbuf[...], (((1,), (1,)), ((), ())), preferred_element_type=F32
        ) + LOGIT_BIAS
        chance = jax.nn.sigmoid(logits)
        if slot == 0:
            row_ids = lax.broadcasted_iota(jnp.int32, chance.shape, 0)
            col_ids = lax.broadcasted_iota(jnp.int32, chance.shape, 1)
            chance = chance - jnp.where((row_ids == col_ids) & (row_ids < R), 1.0, 0.0)
        coef[rows, :] = (LOGIT_SCALE * chance).astype(BF16)

    def image_sums(slot, count):
        rows = blocks(slot, count)
        ip[rows, :] = jnp.dot(coef[rows, :], tbuf[...], preferred_element_type=F32)

    def text_sums(slot, count, cols):
        rows = blocks(slot, count)
        return lax.dot_general(
            coef[rows, cols], ibuf[rows, :], (((0,), (0,)), ((), ())), preferred_element_type=F32
        )

    def send_b(slot, d1):
        rows = blocks(slot)
        b_out[rows, :] = ip[rows, :].astype(BF16)
        to = {1: "bp", 2: "b2", 3: "bm"}[slot // 4]
        copy_of("bo", ("bo", d1), b_out.at[rows, :], b_in.at[rows, :], to).start()

    coef_of(0, 4)
    for d1 in range(4):
        if d1 in VIA_P:
            got(("i", 12 + d1), ibuf.at[blocks(12 + d1), :])
        else:
            got(("i", 4 + d1), ibuf.at[blocks(4 + d1), :])
    coef_of(4, 4)
    image_sums(4, 4)
    for d1 in (2, 1, 3, 0):
        send_b(4 + d1, d1)
    coef_of(12, 4)
    image_sums(12, 4)
    for d1 in (2, 1, 3, 0):
        send_b(12 + d1, d1)
    thirds = [pl.ds(n * 256, 256) for n in range(3)]
    for cols in thirds:
        tp[cols, :] = text_sums(0, 8, cols) + text_sums(12, 4, cols)
    image_sums(0, 4)

    got("far", ibuf.at[blocks(8, 4), :])
    coef_of(8, 4)

    def send_so(k):
        rows = blocks(k)
        sib_out[rows, :] = tp[blocks(8 + k), :].astype(BF16)
        copy_of("so", ("so", k), sib_out.at[rows, :], sib_in.at[rows, :], "sib").start()

    for cols in (thirds[2], thirds[1], thirds[0]):
        tp[cols, :] += text_sums(8, 4, cols)
    for k in (4, 5, 3, 6, 2, 7, 1, 0):
        send_so(k)
    image_sums(8, 4)
    for d1 in (2, 1, 3, 0):
        send_b(8 + d1, d1)

    def b_sum(d1):
        got(("bo", d1), b_in.at[blocks(0, 3), :])
        total = ip[blocks(d1), :]
        for d2 in (1, 2, 3):
            total = total + b_in[blocks(4 * d2 + d1), :].astype(F32)
        return total

    def z_pass(k, to, new):
        got(("so", k), sib_in.at[blocks(k), :])
        for p in pieces:
            rows = rows_of(k, p)
            total = tp[rows, :] + sib_in[rows, :].astype(F32)
            if k not in (4, 5):
                got(("zo", k, p), z_in.at[rows, :])
                total = total + z_in[rows, :].astype(F32)
            z_out[rows, :] = total.astype(BF16)
            key = ("zo", new) if new in (0, 8) else ("zo", new, p)
            slot = 4 if new == 8 else new
            copy_of("zo", key, z_out.at[rows, :], z_in.at[rows_of(slot, p), :], to).start()

    def send_a(d1, to):
        rows = blocks(d1)
        a_out[rows, :] = b_sum(d1).astype(BF16)
        copy_of("ao", "ao", a_out.at[rows, :], a_in.at[rows, :], to).start()

    z_pass(4, "zp", 3)
    z_pass(5, "zm", 6)
    z_pass(3, "zp", 2)
    z_pass(6, "zm", 7)
    send_a(2, "a2")
    z_pass(2, "zp", 1)
    z_pass(7, "zm", 8)
    send_a(1, "ap")
    send_a(3, "am")
    z_pass(1, "zp", 0)

    def back_norm(unit_rows, scale, direction):
        inner = jnp.sum(unit_rows * direction, axis=-1, keepdims=True)
        return scale * (direction - unit_rows * inner)

    total = b_sum(0)
    got("ao", a_in.at[blocks(0, 3), :])
    for d1 in (1, 2, 3):
        total = total + a_in[blocks(d1), :].astype(F32)
    image_grad = back_norm(iunit[...], iscale[:, :1], total)
    for j in range(4):
        g_out[j] = image_grad[:, j * Q:(j + 1) * Q].astype(BF16)
    for step in (1, 2, 3):
        copy_of("g", "g", g_out.at[(grp + step) % 4], g_in.at[grp], "g%d" % step).start()
    keep = pltpu.make_async_copy(g_out.at[grp], g_in.at[grp], local_sems.at[2])
    keep.start()

    got(("so", 0), sib_in.at[blocks(0), :])
    got(("zo", 0), z_in.at[blocks(0), :])
    got(("zo", 8), z_in.at[blocks(4), :])
    direction = tp[blocks(0), :] + sib_in[blocks(0), :].astype(F32)
    direction = direction + z_in[blocks(0), :].astype(F32) + z_in[blocks(4), :].astype(F32)
    text_unit, text_scale = unit_of(tin[...].astype(F32))
    otxt[...] = back_norm(text_unit, text_scale, direction).astype(BF16)

    left("x", xin.at[pl.ds(0, 3)])
    left("t", tbuf.at[blocks(0, 7), :])
    left("s", tbuf.at[blocks(0, 8), :])
    left("i", ibuf.at[blocks(0, 15), :])
    left("so", sib_out)
    left("bo", b_out.at[blocks(0, 12), :])
    left("zo", z_out.at[blocks(0, 7), :])
    left("ao", a_out.at[blocks(0, 3), :])
    keep.wait()
    got("g", g_in.at[pl.ds(0, 3)])
    for j in range(4):
        oimg[pl.ds(j * R, R), :] = g_in[j]
    left("g", g_out.at[pl.ds(0, 3)])
    assert (len(send_ids), len(recv_ids)) == (SENDS, RECVS), (len(send_ids), len(recv_ids))


def on_device(image_features, text_features):
    vmem = pltpu.VMEM
    return pl.pallas_call(
        kernel,
        out_shape=(
            jax.ShapeDtypeStruct((4 * R, Q), BF16),
            jax.ShapeDtypeStruct((R, D), BF16),
        ),
        in_specs=[pl.BlockSpec(memory_space=pl.ANY)] * 2,
        out_specs=(pl.BlockSpec(memory_space=vmem), pl.BlockSpec(memory_space=vmem)),
        scratch_shapes=[
            vmem((4, R, Q), BF16),
            vmem((R, D), BF16),
            vmem((N, D), BF16),
            vmem((N, D), BF16),
            vmem((N, N), BF16),
            vmem((N, D), F32),
            vmem((N, D), F32),
            vmem((R, 128), F32),
            vmem((R, D), F32),
            vmem((8 * R, D), BF16),
            vmem((8 * R, D), BF16),
            vmem((8 * R, D), BF16),
            vmem((8 * R, D), BF16),
            vmem((N, D), BF16),
            vmem((N, D), BF16),
            vmem((4 * R, D), BF16),
            vmem((4 * R, D), BF16),
            vmem((4, R, Q), BF16),
            vmem((4, R, Q), BF16),
            pltpu.SemaphoreType.DMA((SENDS,)),
            pltpu.SemaphoreType.DMA((RECVS,)),
            pltpu.SemaphoreType.DMA((3,)),
        ],
        compiler_params=pltpu.CompilerParams(
            collective_id=0, has_side_effects=True, vmem_limit_bytes=60 * 1024 * 1024
        ),
        cost_estimate=pl.CostEstimate(
            flops=6 * N * N * D, bytes_accessed=8 * R * D, transcendentals=N * N
        ),
    )(image_features, text_features)


def solution(mesh):
    placed = (P("loop", "grp"), P(("loop", "grp"), None))
    return jax.shard_map(
        on_device, mesh=mesh, in_specs=placed, out_specs=placed, check_vma=False
    )
```

time: 65.2 us -> 56.9 us (0.87)
  Pallas kernels: 61.3 us -> 53.9 us
  local copies, waits for them, and re-layouts: 3.11 us -> 2.27 us
    pallas_call x1, Pallas kernels: 61.3 us -> 53.9 us  [on_device(): pl.pallas_call(kernel, out_shape=(jax.ShapeDtypeStruct((4 * R, Q), BF16),...]
    unnamed x6 -> x4, local copies, waits for them, and re-layouts: 3.11 us -> 2.27 us
where the time goes in v2:
time: 56.9 us; the launch traced here: 56.8 us
  Pallas kernels  53.9 us (95%)
  local copies, waits for them, and re-layouts  2.27 us (4%)
  between operations  0.65 us (1%)
    pallas_call x1, Pallas kernels, on_device(): pl.pallas_call(kernel, out_shape=(jax.ShapeDtypeStruct((4 * R, Q), BF16),...  53.9 us
    unnamed x4, local copies, waits for them, and re-layouts  2.27 us

profile of v2, /device:TPU:1, one launch (start us, length us, event | category | flops | bytes accessed | tf_op | source)
XLA Modules:
  0.0 56.8 jit_solution(8016794042471621810)
XLA Ops:
  0.6 53.9 %shard_map.41 = (bf16[192,288]{1,0:T(8,128)(2,1)}, bf16[48,1152]{1,0:T(8,128)(2,1)}) custom-call(bf16[192,288]{1,0:T(8,128)(2,1)} %img.1, bf16[48,1152]{1,0:T(8,128)(2,1)} %txt.1), custom_call_target="tpu_custom_call" | custom-call | flops 4076863488 | bytes 442368 | tf_op jit(solution)/shard_map/pallas_call | solution.py:335
  54.5 0.0 copy-start
  54.5 1.6 %copy.6 = bf16[192,288]{1,0:T(8,128)(2,1)} copy(bf16[192,288]{1,0:T(8,128)(2,1)} %get-tuple-element.4) | data formatting | bytes 221184
  56.1 0.0 copy-done
  56.1 0.6 %copy.7 = bf16[48,1152]{1,0:T(8,128)(2,1)} copy(bf16[48,1152]{1,0:T(8,128)(2,1)S(1)} %copy-done) | data formatting | bytes 221184
Async XLA Ops:
  54.5 1.6 %copy-start = (bf16[48,1152]{1,0:T(8,128)(2,1)S(1)}, bf16[48,1152]{1,0:T(8,128)(2,1)}, u32[]{:S(2)}) copy-start(bf16[48,1152]{1,0:T(8,128)(2,1)} %get-tuple-element.5) | copy-start | bytes 331780

commit v3 on v2

v3 whole, which is shorter than its diff:
```python
import jax
import jax.numpy as jnp
from jax import lax
from jax.experimental import pallas as pl
from jax.experimental.pallas import tpu as pltpu
from jax.sharding import PartitionSpec as P

LOGIT_SCALE = 16.0
LOGIT_BIAS = -4.0
BF16 = jnp.bfloat16
F32 = jnp.float32
H = 96
R = 48
D = 1152
Q = 288
N = 768
PIECES = 3
PR = R // PIECES
SENDS = 10
RECVS = 64
GREETED = ("zp", "zm", "zp2", "zm2", "ap", "am", "bp", "bm", "y2", "g1", "g2", "g3")
MESH = pl.DeviceIdType.MESH
FORWARD = (0, 1, 3, 2)
OWN = {0: 0, 1: 1, 7: 2, 2: 3, 6: 4, 3: 10, 5: 11, 4: 12}
OTHER = {k: place + (5 if place < 5 else 3) for k, place in OWN.items()}
EARLY = 10 * R
LATE = N - EARLY
VIA_P = (0, 2)


def neighbours():
    loop = lax.axis_index("loop")
    grp = lax.axis_index("grp")
    z = loop // 8
    x = (grp // 2) * 2 + (loop // 4) % 2
    y = loop % 4
    c = grp % 2

    def dev(dz, dx, dy, flip=0):
        zz = (z + dz + 8) % 8
        xx = (x + dx + 4) % 4
        yy = (y + dy + 4) % 4
        return (zz * 8 + (xx % 2) * 4 + yy, (xx // 2) * 2 + (c + flip) % 2)

    f = 1 - 2 * c
    return {
        "zp": dev(f, 0, 0),
        "zm": dev(-f, 0, 0),
        "zp2": dev(2 * f, 0, 0),
        "zm2": dev(-2 * f, 0, 0),
        "ap": dev(0, 1 - c, c),
        "am": dev(0, c - 1, -c),
        "bp": dev(0, c, 1 - c),
        "bm": dev(0, -c, c - 1),
        "a2": dev(0, 2 - 2 * c, 2 * c),
        "b2": dev(0, 2 * c, 2 - 2 * c),
        "y2": dev(0, 0, 2),
        "sib": dev(0, 0, 0, 1),
        "g1": (loop, (grp + 1) % 4),
        "g2": (loop, (grp + 2) % 4),
        "g3": (loop, (grp + 3) % 4),
    }, grp, x, c


def unit_of(values):
    scale = lax.rsqrt(jnp.sum(values * values, axis=-1, keepdims=True) + 1e-06)
    return values * scale, scale


def permuted(values):
    mains = [values[:, q * Q:q * Q + 256] for q in range(4)]
    return jnp.concatenate(mains + [values[:, q * Q + 256:(q + 1) * Q] for q in range(4)], axis=1)


def quarter(values, q):
    return jnp.concatenate(
        [values[:, q * 256:(q + 1) * 256], values[:, 1024 + q * 32:1024 + (q + 1) * 32]], axis=1
    )


def kernel(
    img, txt, oimg, otxt,
    ximg, xrem, srem, rmain, rrem, tin, ibuf, tbuf, coef_early, coef_late, ip, tp,
    sib_out, sib_in, z_out, z_in, b_out, b_in, a_out, a_in, g_out, g_in,
    send_sems, recv_sems, local_sems,
):
    dev, grp, x, c = neighbours()
    xh = x // 2
    send_ids = {}
    recv_ids = {}

    def copy_of(kind, key, src, dst, to):
        out = send_ids.setdefault(kind, len(send_ids))
        arrive = recv_ids.setdefault(key, len(recv_ids))
        return pltpu.make_async_remote_copy(
            src_ref=src, dst_ref=dst, send_sem=send_sems.at[out],
            recv_sem=recv_sems.at[arrive], device_id=dev[to], device_id_type=MESH,
        )

    def got(key, ref):
        pltpu.make_async_copy(ref, ref, recv_sems.at[recv_ids[key]]).wait()

    def left(kind, ref):
        pltpu.make_async_copy(ref, ref, send_sems.at[send_ids[kind]]).wait()

    def blocks(slot, count=1):
        return pl.ds(slot * R, count * R)

    def rows_of(slot, piece):
        return pl.ds(slot * R + piece * PR, PR)

    pieces = range(PIECES)
    load_t = pltpu.make_async_copy(txt, tin, local_sems.at[0])
    load_t.start()
    load_i = pltpu.make_async_copy(img, ximg, local_sems.at[1])
    load_i.start()

    barrier = pltpu.get_barrier_semaphore()
    for name in GREETED:
        pl.semaphore_signal(barrier, inc=1, device_id=dev[name], device_id_type=MESH)
    load_t.wait()
    unit, tscale = unit_of(permuted(tin[...].astype(F32)))
    tbuf[blocks(0), :] = unit.astype(BF16)
    load_i.wait()

    def rest_of(half):
        rest = ximg[pl.ds(pl.multiple_of(half * H, 32), H), 256:].astype(F32)
        low, high = rest[:R], rest[R:]
        gap = jnp.zeros_like(low)
        return jnp.where(
            c == 0,
            jnp.concatenate([low, gap, high, gap], axis=1),
            jnp.concatenate([gap, low, gap, high], axis=1),
        )

    xrem[...] = rest_of(1 - c).astype(BF16)
    rest_here = rest_of(c)
    there = pl.ds(pl.multiple_of((1 - c) * H, 32), H)
    here = pl.ds(pl.multiple_of(c * H, 32), H)
    rmain[grp, pl.ds(4 * H, H), :] = ximg[here, :256]
    pl.semaphore_wait(barrier, len(GREETED))

    copy_of("x", "x", ximg.at[there, pl.ds(0, 256)], rmain.at[grp, pl.ds(4 * H, H), :], "sib").start()
    copy_of("y", "x", xrem, srem, "sib").start()

    def send_t(to, slot, new, piece):
        key = ("t", new) if new in (3, 4, 5) else ("t", new, piece)
        src, dst = rows_of(OWN[slot], piece), rows_of(OWN[new], piece)
        copy_of("t", key, tbuf.at[src, :], tbuf.at[dst, :], to).start()

    def send_s(slot):
        key = "s late" if slot in (3, 5, 4) else "s early"
        src, dst = blocks(OWN[slot]), blocks(OTHER[slot])
        copy_of("s", key, tbuf.at[src, :], tbuf.at[dst, :], "sib").start()

    for p in pieces:
        send_t("zm", 0, 1, p)
        send_t("zp", 0, 7, p)
    send_s(0)

    def slot_of(d1, d2):
        return 4 * (1 - d2 % 2) + (1 - c) * ((d2 // 2) * 2 + d1 % 2) + c * d1

    def half_of(d1, d2):
        return ((x + (1 - c) * d1 + c * d2) % 4) // 2

    def send_i(to, source, target, key):
        half = half_of(*source)
        quarters = pl.ds(2 * half, 2)
        came, goes = slot_of(*source), slot_of(*target)
        src = pl.ds(pl.multiple_of(came * H, 32), H)
        dst = pl.ds(pl.multiple_of(goes * H, 32), H)
        copy_of("i", key, rmain.at[quarters, src, :], rmain.at[quarters, dst, :], to).start()
        src = pl.ds(pl.multiple_of(came * R, 16), R)
        dst = pl.ds(pl.multiple_of(goes * R, 16), R)
        copy_of("i", key, rrem.at[half, src, :], rrem.at[half, dst, :], to).start()

    def got_i(key):
        got(key, tbuf.at[blocks(0), :])

    def near_b(d1):
        send_i("bm", (d1, 0), (d1, 1), ("i", d1, 1))
        send_i("bp", (d1, 0), (d1, 3), ("i", d1, 3))
        if d1 not in FORWARD:
            send_i("b2", (d1, 0), (d1, 2), ("i", d1, 2))

    def far_b(d1):
        if d1 in VIA_P:
            got_i(("i", d1, 1))
            send_i("bm", (d1, 1), (d1, 2), ("i", d1, 2))
        else:
            got_i(("i", d1, 3))
            send_i("bp", (d1, 3), (d1, 2), ("i", d1, 2))

    got("x", rrem.at[0, pl.ds(0, 5 * R), :])
    rrem[xh, pl.ds(4 * R, R), :] = (rest_here + srem[...].astype(F32)).astype(BF16)
    send_i("am", (0, 0), (1, 0), ("i", 1, 0))
    send_i("ap", (0, 0), (3, 0), ("i", 3, 0))
    send_i("a2", (0, 0), (2, 0), ("i", 2, 0))
    near_b(0)

    def ring_t(new_m, new_p):
        for p in pieces:
            got(("t", new_m, p), tbuf.at[rows_of(OWN[new_m], p), :])
            send_t("zm", new_m, new_m + 1, p)
            if new_p == 6:
                send_t("zm2", 2, 4, p)
            got(("t", new_p, p), tbuf.at[rows_of(OWN[new_p], p), :])
            send_t("zp", new_p, new_p - 1, p)
        send_s(new_m)
        send_s(new_p)

    ring_t(1, 7)
    for d1 in (1, 3):
        got_i(("i", d1, 0))
        near_b(d1)
    got_i(("i", 2, 0))
    near_b(2)
    ring_t(2, 6)
    for d1 in FORWARD:
        far_b(d1)

    def late_t(slot):
        got(("t", slot), tbuf.at[blocks(OWN[slot]), :])
        send_s(slot)

    def rests(slot):
        rows = pl.ds(pl.multiple_of(slot * R, 16), R)
        first, second = rrem[0, rows, :].astype(F32), rrem[1, rows, :].astype(F32)
        left_side = lax.broadcasted_iota(jnp.int32, first.shape, 1) < 64
        low = jnp.where(left_side, first, pltpu.roll(second, 64, 1))
        high = jnp.where(left_side, pltpu.roll(first, 64, 1), second)
        return low, high

    def normalise(slot, carry):
        rows = pl.ds(pl.multiple_of(slot * H, 32), H)
        parts = [rmain[q, rows, :].astype(F32) for q in range(4)]
        parts.append(jnp.concatenate(rests(slot), axis=0))
        squares = [jnp.sum(part * part, axis=-1, keepdims=True) for part in parts]
        scale = lax.rsqrt(sum(squares[1:], squares[0]) + 1e-06)
        for q, part in enumerate(parts):
            ibuf[rows, pl.ds(256 * q, part.shape[1])] = (part * scale).astype(BF16)
        return carry

    def normalised(slot, count):
        lax.fori_loop(slot, slot + count, normalise, 0)

    def coef_of(slot, count, part):
        store, texts = part
        rows = pl.ds(slot * H, count * H)
        logits = LOGIT_SCALE * lax.dot_general(
            ibuf[rows, :], tbuf[texts, :], (((1,), (1,)), ((), ())), preferred_element_type=F32
        ) + LOGIT_BIAS
        chance = jax.nn.sigmoid(logits)
        if slot == 4 and part is early:
            row_ids = lax.broadcasted_iota(jnp.int32, chance.shape, 0)
            col_ids = lax.broadcasted_iota(jnp.int32, chance.shape, 1)
            start = OTHER[0] * R
            own = (col_ids < R) & (row_ids == col_ids + c * R)
            other = (col_ids >= start) & (col_ids < start + R) & (row_ids == col_ids - start + (1 - c) * R)
            chance = chance - jnp.where((own | other) & (c == xh), 1.0, 0.0)
        store[rows, :] = (LOGIT_SCALE * chance).astype(BF16)

    def image_sums(slot, count, part):
        store, texts = part
        rows = pl.ds(slot * H, count * H)
        return jnp.dot(store[rows, :], tbuf[texts, :], preferred_element_type=F32)

    def text_sums(slot, count, part):
        rows = pl.ds(slot * H, count * H)
        return lax.dot_general(
            part[0][rows, :], ibuf[rows, :], (((0,), (0,)), ((), ())), preferred_element_type=F32
        )

    early = (coef_early, pl.ds(0, EARLY))
    late = (coef_late, pl.ds(EARLY, LATE))

    def part_of(d1, d2):
        start = slot_of(d1, d2) * H + half_of(d1, d2) * R
        return ip[pl.ds(pl.multiple_of(start, 16), R), :]

    def send_b(d1, d2):
        rows = blocks(4 * d2 + d1)
        b_out[rows, :] = part_of(d1, d2).astype(BF16)
        to = {1: "bp", 2: "b2", 3: "bm"}[d2]
        copy_of("bo", ("bo", d1), b_out.at[rows, :], b_in.at[rows, :], to).start()

    for d1 in range(4):
        for d2 in (1, 3):
            if d1 not in FORWARD or d2 != (1 if d1 in VIA_P else 3):
                got_i(("i", d1, d2))
    first, second, third = pl.ds(0, 4 * H), pl.ds(4 * H, 2 * H), pl.ds(6 * H, 2 * H)
    normalised(0, 4)
    got("s early", tbuf.at[blocks(0, 5), :])
    coef_of(0, 4, early)
    ip[first, :] = image_sums(0, 4, early)
    late_t(3)
    late_t(5)
    for d1 in (0, 1):
        got_i(("i", d1, 2))
    normalised(4, 2)
    coef_of(4, 2, early)
    late_t(4)
    tp[early[1], :] = text_sums(0, 6, early)
    ip[second, :] = image_sums(4, 2, early)

    got("s late", tbuf.at[blocks(0, 3), :])
    coef_of(0, 4, late)
    ip[first, :] += image_sums(0, 4, late)
    for d1 in (2, 1, 3, 0):
        for d2 in (1, 3):
            send_b(d1, d2)
    coef_of(4, 2, late)
    for d1 in (2, 3):
        got_i(("i", d1, 2))
    normalised(6, 2)
    coef_of(6, 2, late)
    coef_of(6, 2, early)

    def send_so(k):
        rows = blocks(k)
        sib_out[rows, :] = tp[blocks(OTHER[k]), :].astype(BF16)
        copy_of("so", ("so", k), sib_out.at[rows, :], sib_in.at[rows, :], "sib").start()

    tp[late[1], :] = text_sums(0, 8, late)
    for k in (4, 5, 3):
        send_so(k)
    tp[early[1], :] += text_sums(6, 2, early)
    for k in (6, 2, 7, 1, 0):
        send_so(k)
    ip[second, :] += image_sums(4, 2, late)
    ip[third, :] = image_sums(6, 2, early) + image_sums(6, 2, late)
    for d1 in (2, 1, 3, 0):
        send_b(d1, 2)

    def b_sum(d1):
        got(("bo", d1), b_in.at[blocks(0, 3), :])
        total = part_of(d1, 0)
        for d2 in (1, 2, 3):
            total = total + b_in[blocks(4 * d2 + d1), :].astype(F32)
        return total

    def z_pass(k, to, new):
        got(("so", k), sib_in.at[blocks(k), :])
        for p in pieces:
            rows = rows_of(k, p)
            total = tp[rows_of(OWN[k], p), :] + sib_in[rows, :].astype(F32)
            if k not in (4, 5):
                got(("zo", k, p), z_in.at[rows, :])
                total = total + z_in[rows, :].astype(F32)
            z_out[rows, :] = total.astype(BF16)
            key = ("zo", new) if new in (0, 8) else ("zo", new, p)
            slot = 4 if new == 8 else new
            copy_of("zo", key, z_out.at[rows, :], z_in.at[rows_of(slot, p), :], to).start()

    def send_a(d1, to):
        rows = blocks(d1)
        a_out[rows, :] = b_sum(d1).astype(BF16)
        copy_of("ao", "ao", a_out.at[rows, :], a_in.at[rows, :], to).start()

    z_pass(4, "zp", 3)
    z_pass(5, "zm", 6)
    z_pass(3, "zp", 2)
    z_pass(6, "zm", 7)
    send_a(2, "a2")
    z_pass(2, "zp", 1)
    z_pass(7, "zm", 8)
    send_a(1, "ap")
    send_a(3, "am")
    z_pass(1, "zp", 0)

    def back_norm(unit_rows, scale, direction):
        inner = jnp.sum(unit_rows * direction, axis=-1, keepdims=True)
        return scale * (direction - unit_rows * inner)

    total = b_sum(0)
    got("ao", a_in.at[blocks(0, 3), :])
    for d1 in (1, 2, 3):
        total = total + a_in[blocks(d1), :].astype(F32)
    own_rows = pl.ds(pl.multiple_of(4 * H + xh * R, 16), R)
    low, high = rests(4)
    own_parts = [rmain[q, own_rows, :].astype(F32) for q in range(4)]
    image_unit, image_scale = unit_of(jnp.concatenate(own_parts + [jnp.where(xh == 0, low, high)], axis=1))
    image_grad = back_norm(image_unit, image_scale, total)
    for j in range(4):
        g_out[j] = quarter(image_grad, j).astype(BF16)
    for step in (1, 2, 3):
        copy_of("g", "g", g_out.at[(grp + step) % 4], g_in.at[grp], "g%d" % step).start()
    keep = pltpu.make_async_copy(g_out.at[grp], g_in.at[grp], local_sems.at[2])
    keep.start()

    got(("so", 0), sib_in.at[blocks(0), :])
    got(("zo", 0), z_in.at[blocks(0), :])
    got(("zo", 8), z_in.at[blocks(4), :])
    direction = tp[blocks(0), :] + sib_in[blocks(0), :].astype(F32)
    direction = direction + z_in[blocks(0), :].astype(F32) + z_in[blocks(4), :].astype(F32)
    text_unit, text_scale = unit_of(permuted(tin[...].astype(F32)))
    text_grad = back_norm(text_unit, text_scale, direction)
    otxt[...] = jnp.concatenate([quarter(text_grad, j) for j in range(4)], axis=1).astype(BF16)

    left("x", rmain.at[0, pl.ds(0, H), :])
    left("y", xrem)
    left("t", tbuf.at[blocks(0, 7), :])
    left("s", tbuf.at[blocks(0, 8), :])
    left("i", ibuf.at[blocks(0, 15), :])
    left("so", sib_out)
    left("bo", b_out.at[blocks(0, 12), :])
    left("zo", z_out.at[blocks(0, 7), :])
    left("ao", a_out.at[blocks(0, 3), :])
    keep.wait()
    got("g", g_in.at[pl.ds(0, 3)])
    for j in range(4):
        oimg[pl.ds((j % 2) * H + (j // 2) * R, R), :] = g_in[j]
    left("g", g_out.at[pl.ds(0, 3)])
    assert (len(send_ids), len(recv_ids)) == (SENDS, RECVS), (len(send_ids), len(recv_ids))


def on_device(image_features, text_features):
    vmem = pltpu.VMEM
    return pl.pallas_call(
        kernel,
        out_shape=(
            jax.ShapeDtypeStruct((4 * R, Q), BF16),
            jax.ShapeDtypeStruct((R, D), BF16),
        ),
        in_specs=[pl.BlockSpec(memory_space=pl.ANY)] * 2,
        out_specs=(pl.BlockSpec(memory_space=vmem), pl.BlockSpec(memory_space=vmem)),
        scratch_shapes=[
            vmem((4 * R, Q), BF16),
            vmem((R, 128), BF16),
            vmem((R, 128), BF16),
            vmem((4, N, 256), BF16),
            vmem((2, N // 2, 128), BF16),
            vmem((R, D), BF16),
            vmem((N, D), BF16),
            vmem((N, D), BF16),
            vmem((N, EARLY), BF16),
            vmem((N, LATE), BF16),
            vmem((N, D), F32),
            vmem((N, D), F32),
            vmem((8 * R, D), BF16),
            vmem((8 * R, D), BF16),
            vmem((8 * R, D), BF16),
            vmem((8 * R, D), BF16),
            vmem((N, D), BF16),
            vmem((N, D), BF16),
            vmem((4 * R, D), BF16),
            vmem((4 * R, D), BF16),
            vmem((4, R, Q), BF16),
            vmem((4, R, Q), BF16),
            pltpu.SemaphoreType.DMA((SENDS,)),
            pltpu.SemaphoreType.DMA((RECVS,)),
            pltpu.SemaphoreType.DMA((3,)),
        ],
        compiler_params=pltpu.CompilerParams(
            collective_id=0, has_side_effects=True, vmem_limit_bytes=60 * 1024 * 1024
        ),
        cost_estimate=pl.CostEstimate(
            flops=6 * N * N * D, bytes_accessed=8 * R * D, transcendentals=N * N
        ),
    )(image_features, text_features)


def solution(mesh):
    placed = (P("loop", "grp"), P(("loop", "grp"), None))
    return jax.shard_map(
        on_device, mesh=mesh, in_specs=placed, out_specs=placed, check_vma=False
    )
```

time: 56.9 us -> 53.5 us (0.940)
  Pallas kernels: 53.9 us -> 50.5 us
    pallas_call x1, Pallas kernels: 53.9 us -> 50.5 us  [on_device(): pl.pallas_call(kernel, out_shape=(jax.ShapeDtypeStruct((4 * R, Q), BF16),...]
where the time goes in v3:
time: 53.5 us; the launch traced here: 53.4 us
  Pallas kernels  50.5 us (94%)
  local copies, waits for them, and re-layouts  2.27 us (4%)
  between operations  0.65 us (1%)
    pallas_call x1, Pallas kernels, on_device(): pl.pallas_call(kernel, out_shape=(jax.ShapeDtypeStruct((4 * R, Q), BF16),...  50.5 us
    unnamed x4, local copies, waits for them, and re-layouts  2.27 us

profile of v3, /device:TPU:1, one launch (start us, length us, event | category | flops | bytes accessed | tf_op | source)
XLA Modules:
  0.0 53.4 jit_solution(9324100703821740796)
XLA Ops:
  0.6 50.5 %shard_map.41 = (bf16[192,288]{1,0:T(8,128)(2,1)}, bf16[48,1152]{1,0:T(8,128)(2,1)}) custom-call(bf16[192,288]{1,0:T(8,128)(2,1)} %img.1, bf16[48,1152]{1,0:T(8,128)(2,1)} %txt.1), custom_call_target="tpu_custom_call" | custom-call | flops 4076863488 | bytes 442368 | tf_op jit(solution)/shard_map/pallas_call | solution.py:420
  51.1 0.0 copy-start
  51.1 1.6 %copy.6 = bf16[192,288]{1,0:T(8,128)(2,1)} copy(bf16[192,288]{1,0:T(8,128)(2,1)} %get-tuple-element.4) | data formatting | bytes 221184
  52.7 0.0 copy-done
  52.7 0.6 %copy.7 = bf16[48,1152]{1,0:T(8,128)(2,1)} copy(bf16[48,1152]{1,0:T(8,128)(2,1)S(1)} %copy-done) | data formatting | bytes 221184
Async XLA Ops:
  51.1 1.6 %copy-start = (bf16[48,1152]{1,0:T(8,128)(2,1)S(1)}, bf16[48,1152]{1,0:T(8,128)(2,1)}, u32[]{:S(2)}) copy-start(bf16[48,1152]{1,0:T(8,128)(2,1)} %get-tuple-element.5) | copy-start | bytes 331780

commit v4 on v3

--- a/solution.py
+++ b/solution.py
@@ -16,9 +16,9 @@
 N = 768
 PIECES = 3
 PR = R // PIECES
-SENDS = 10
-RECVS = 64
-GREETED = ("zp", "zm", "zp2", "zm2", "ap", "am", "bp", "bm", "y2", "g1", "g2", "g3")
+SENDS = 13
+RECVS = 66
+GREETED = ("zp", "zm", "zp2", "zm2", "ap", "am", "bp", "bm", "x2", "y2", "sib")
 MESH = pl.DeviceIdType.MESH
 FORWARD = (0, 1, 3, 2)
 OWN = {0: 0, 1: 1, 7: 2, 2: 3, 6: 4, 3: 10, 5: 11, 4: 12}
@@ -54,11 +54,9 @@
         "bm": dev(0, -c, c - 1),
         "a2": dev(0, 2 - 2 * c, 2 * c),
         "b2": dev(0, 2 * c, 2 - 2 * c),
+        "x2": dev(0, 2, 0),
         "y2": dev(0, 0, 2),
         "sib": dev(0, 0, 0, 1),
-        "g1": (loop, (grp + 1) % 4),
-        "g2": (loop, (grp + 2) % 4),
-        "g3": (loop, (grp + 3) % 4),
     }, grp, x, c
 
 
@@ -80,8 +78,9 @@
 
 def kernel(
     img, txt, oimg, otxt,
-    ximg, xrem, srem, rmain, rrem, tin, ibuf, tbuf, coef_early, coef_late, ip, tp,
-    sib_out, sib_in, z_out, z_in, b_out, b_in, a_out, a_in, g_out, g_in,
+    ximg, xrem, srem, rmain, rrem, tin, tunit, tscales, ibuf, tbuf, coef_early, coef_late, ip, tp,
+    sib_out, sib_in, z_out, z_in, b_main, b_rest, b_main_in, b_rest_in, a_main, a_rest, a_main_in, a_rest_in,
+    inner_sums, inner_slots, b_inner, b_inner_in, a_inner, a_inner_in, g_main, g_rest, g_main_in, g_rest_in,
     send_sems, recv_sems, local_sems,
 ):
     dev, grp, x, c = neighbours()
@@ -121,6 +120,9 @@
     load_t.wait()
     unit, tscale = unit_of(permuted(tin[...].astype(F32)))
     tbuf[blocks(0), :] = unit.astype(BF16)
+    tunit[...] = unit
+    tscales[...] = jnp.broadcast_to(tscale, (R, 128))
+    inner_sums[...] = jnp.zeros_like(inner_sums)
     load_i.wait()
 
     def rest_of(half):
@@ -275,15 +277,51 @@
     early = (coef_early, pl.ds(0, EARLY))
     late = (coef_late, pl.ds(EARLY, LATE))
 
-    def part_of(d1, d2):
-        start = slot_of(d1, d2) * H + half_of(d1, d2) * R
-        return ip[pl.ds(pl.multiple_of(start, 16), R), :]
+    left_side = lax.broadcasted_iota(jnp.int32, (R, 128), 1) < 64
+
+    def shard_of(d1, d2):
+        rows = pl.ds(pl.multiple_of(slot_of(d1, d2) * H, 32), H)
+        half = half_of(d1, d2)
+        main = ip[rows, pl.ds(pl.multiple_of(half * 512, 512), 512)]
+        low, high = ip[rows, pl.ds(1024, 128)][:R], ip[rows, pl.ds(1024, 128)][R:]
+        rest = jnp.where(
+            half == 0,
+            jnp.where(left_side, low, pltpu.roll(high, 64, 1)),
+            jnp.where(left_side, pltpu.roll(low, 64, 1), high),
+        )
+        return main, rest
+
+    def send_shard(kind, key, place, shard, mains, rests_out, mains_in, rests_in, to):
+        rows = pl.ds(place * H, H)
+        mains[rows, :] = shard[0].astype(BF16)
+        copy_of(kind, key, mains.at[rows, :], mains_in.at[rows, :], to).start()
+        rows = blocks(place)
+        rests_out[rows, :] = shard[1].astype(BF16)
+        copy_of(kind, key, rests_out.at[rows, :], rests_in.at[rows, :], to).start()
+
+    def add_shard(shard, place, mains_in, rests_in):
+        return (
+            shard[0] + mains_in[pl.ds(place * H, H), :].astype(F32),
+            shard[1] + rests_in[blocks(place), :].astype(F32),
+        )
 
     def send_b(d1, d2):
-        rows = blocks(4 * d2 + d1)
-        b_out[rows, :] = part_of(d1, d2).astype(BF16)
         to = {1: "bp", 2: "b2", 3: "bm"}[d2]
-        copy_of("bo", ("bo", d1), b_out.at[rows, :], b_in.at[rows, :], to).start()
+        shard = shard_of(d1, d2)
+        send_shard("bo", ("bo", d1), 4 * d2 + d1, shard, b_main, b_rest, b_main_in, b_rest_in, to)
+
+    def raw_inner(slot, carry):
+        rows = pl.ds(pl.multiple_of(slot * H, 32), H)
+        total = jnp.concatenate(rests(slot), axis=0) * ip[rows, pl.ds(1024, 128)]
+        for q in range(4):
+            product = rmain[q, rows, :].astype(F32) * ip[rows, pl.ds(256 * q, 256)]
+            total = total + product[:, :128] + product[:, 128:]
+        high = total.astype(BF16)
+        low = (total - high.astype(F32)).astype(BF16)
+        rows = pl.ds(pl.multiple_of(slot * 128, 128), H)
+        inner_sums[rows, pl.ds(0, 128)] = high
+        inner_sums[rows, pl.ds(128, 128)] = low
+        return carry
 
     for d1 in range(4):
         for d2 in (1, 3):
@@ -328,75 +366,117 @@
     tp[early[1], :] += text_sums(6, 2, early)
     for k in (6, 2, 7, 1, 0):
         send_so(k)
-    ip[second, :] += image_sums(4, 2, late)
-    ip[third, :] = image_sums(6, 2, early) + image_sums(6, 2, late)
-    for d1 in (2, 1, 3, 0):
-        send_b(d1, 2)
-
-    def b_sum(d1):
-        got(("bo", d1), b_in.at[blocks(0, 3), :])
-        total = part_of(d1, 0)
-        for d2 in (1, 2, 3):
-            total = total + b_in[blocks(4 * d2 + d1), :].astype(F32)
-        return total
-
     def z_pass(k, to, new):
         got(("so", k), sib_in.at[blocks(k), :])
         for p in pieces:
             rows = rows_of(k, p)
             total = tp[rows_of(OWN[k], p), :] + sib_in[rows, :].astype(F32)
-            if k not in (4, 5):
-                got(("zo", k, p), z_in.at[rows, :])
-                total = total + z_in[rows, :].astype(F32)
+            for came in (k,) if k not in (4, 5) else ():
+                place = rows_of(came, p)
+                got(("zo", came, p), z_in.at[place, :])
+                total = total + z_in[place, :].astype(F32)
             z_out[rows, :] = total.astype(BF16)
             key = ("zo", new) if new in (0, 8) else ("zo", new, p)
             slot = 4 if new == 8 else new
             copy_of("zo", key, z_out.at[rows, :], z_in.at[rows_of(slot, p), :], to).start()
 
-    def send_a(d1, to):
-        rows = blocks(d1)
-        a_out[rows, :] = b_sum(d1).astype(BF16)
-        copy_of("ao", "ao", a_out.at[rows, :], a_in.at[rows, :], to).start()
-
     z_pass(4, "zp", 3)
     z_pass(5, "zm", 6)
+    ip[second, :] += image_sums(4, 2, late)
+    ip[third, :] = image_sums(6, 2, early) + image_sums(6, 2, late)
+    for d1 in (2, 1, 3, 0):
+        send_b(d1, 2)
+
+    def b_sum(d1):
+        got(("bo", d1), tbuf.at[blocks(0, 3), :])
+        shard = shard_of(d1, 0)
+        for d2 in (1, 2, 3):
+            shard = add_shard(shard, 4 * d2 + d1, b_main_in, b_rest_in)
+        return shard
+
+    def send_a(d1, to):
+        send_shard("ao", "ao", d1, b_sum(d1), a_main, a_rest, a_main_in, a_rest_in, to)
+
+    def inner_b():
+        lax.fori_loop(0, 8, raw_inner, 0)
+        along = lax.dot_general(
+            jnp.ones((8, 256), BF16), inner_sums[...], (((1,), (1,)), ((), ())), preferred_element_type=F32
+        )
+        for slot in range(8):
+            inner_slots[slot] = along[:, slot * 128:(slot + 1) * 128]
+        for d2 in (1, 2, 3):
+            for d1 in range(4):
+                b_inner[4 * d2 + d1] = inner_slots[slot_of(d1, d2)]
+            four = pl.ds(4 * d2, 4)
+            to = {1: "bp", 2: "b2", 3: "bm"}[d2]
+            copy_of("bi", "bi", b_inner.at[four], b_inner_in.at[four], to).start()
+
+    def inner_sum(d1):
+        return inner_slots[slot_of(d1, 0)] + b_inner_in[4 + d1] + b_inner_in[8 + d1] + b_inner_in[12 + d1]
+
+    def inner_a():
+        got("bi", b_inner.at[pl.ds(4, 12)])
+        for d1, to in ((1, "ap"), (2, "a2"), (3, "am")):
+            a_inner[d1] = inner_sum(d1)
+            copy_of("ai", "ai", a_inner.at[d1], a_inner_in.at[d1], to).start()
+
     z_pass(3, "zp", 2)
     z_pass(6, "zm", 7)
+    inner_b()
     send_a(2, "a2")
     z_pass(2, "zp", 1)
     z_pass(7, "zm", 8)
     send_a(1, "ap")
     send_a(3, "am")
+    inner_a()
     z_pass(1, "zp", 0)
 
-    def back_norm(unit_rows, scale, direction):
-        inner = jnp.sum(unit_rows * direction, axis=-1, keepdims=True)
+    def back_norm(unit_rows, scale, inner, direction):
         return scale * (direction - unit_rows * inner)
 
-    total = b_sum(0)
-    got("ao", a_in.at[blocks(0, 3), :])
-    for d1 in (1, 2, 3):
-        total = total + a_in[blocks(d1), :].astype(F32)
-    own_rows = pl.ds(pl.multiple_of(4 * H + xh * R, 16), R)
-    low, high = rests(4)
-    own_parts = [rmain[q, own_rows, :].astype(F32) for q in range(4)]
-    image_unit, image_scale = unit_of(jnp.concatenate(own_parts + [jnp.where(xh == 0, low, high)], axis=1))
-    image_grad = back_norm(image_unit, image_scale, total)
-    for j in range(4):
-        g_out[j] = quarter(image_grad, j).astype(BF16)
-    for step in (1, 2, 3):
-        copy_of("g", "g", g_out.at[(grp + step) % 4], g_in.at[grp], "g%d" % step).start()
-    keep = pltpu.make_async_copy(g_out.at[grp], g_in.at[grp], local_sems.at[2])
-    keep.start()
+    own_rows = pl.ds(4 * H, H)
+    squares = jnp.concatenate(rests(4), axis=0) ** 2
+    for q in range(4):
+        part = rmain[q, own_rows, :].astype(F32)
+        squares = squares + part[:, :128] ** 2 + part[:, 128:] ** 2
+    scale_i = lax.rsqrt(jnp.sum(squares, axis=-1, keepdims=True) + 1e-06)
+    unit_main = jnp.concatenate([rmain[2 * xh + i, own_rows, :].astype(F32) for i in (0, 1)], axis=1) * scale_i
+    scale_rest = jnp.where(left_side, scale_i[:R], scale_i[R:])
+    unit_rest = rrem[xh, blocks(4), :].astype(F32) * scale_rest
+    got("ai", a_inner.at[pl.ds(1, 3)])
+    along = inner_sum(0) + a_inner_in[1] + a_inner_in[2] + a_inner_in[3]
+    inner_i = scale_i * jnp.transpose(jnp.broadcast_to(along[:1], (128, 128)))[:H, :1]
+    inner_rest = jnp.where(left_side, inner_i[:R], inner_i[R:])
 
     got(("so", 0), sib_in.at[blocks(0), :])
     got(("zo", 0), z_in.at[blocks(0), :])
     got(("zo", 8), z_in.at[blocks(4), :])
     direction = tp[blocks(0), :] + sib_in[blocks(0), :].astype(F32)
     direction = direction + z_in[blocks(0), :].astype(F32) + z_in[blocks(4), :].astype(F32)
-    text_unit, text_scale = unit_of(permuted(tin[...].astype(F32)))
-    text_grad = back_norm(text_unit, text_scale, direction)
+    text_unit, text_scale = tunit[...], tscales[:, :1]
+    text_inner = jnp.sum(text_unit * direction, axis=-1, keepdims=True)
+    text_grad = back_norm(text_unit, text_scale, text_inner, direction)
     otxt[...] = jnp.concatenate([quarter(text_grad, j) for j in range(4)], axis=1).astype(BF16)
+
+    shard = b_sum(0)
+    got("ao", tbuf.at[blocks(0, 3), :])
+    for d1 in (1, 2, 3):
+        shard = add_shard(shard, d1, a_main_in, a_rest_in)
+    grad = back_norm(unit_main, scale_i, inner_i, shard[0]).astype(BF16)
+    g_main[0] = grad[:, :256]
+    g_main[1] = grad[:, 256:]
+    g_rest[...] = back_norm(unit_rest, scale_rest, inner_rest, shard[1]).astype(BF16)
+    copy_of("g", "g", g_main.at[1 - c], g_main_in, "sib").start()
+    copy_of("h", "g", g_rest, g_rest_in, "sib").start()
+
+    def put_image(rows, main, rest):
+        rest = rest.astype(F32)
+        low = jnp.where(c == 0, rest[:, :32], rest[:, 32:64])
+        high = jnp.where(c == 0, rest[:, 64:96], rest[:, 96:])
+        oimg[rows, pl.ds(0, 256)] = main
+        oimg[rows, pl.ds(256, 32)] = jnp.concatenate([low, high], axis=0).astype(BF16)
+
+    put_image(here, g_main[c], g_rest[...])
 
     left("x", rmain.at[0, pl.ds(0, H), :])
     left("y", xrem)
@@ -404,14 +484,15 @@
     left("s", tbuf.at[blocks(0, 8), :])
     left("i", ibuf.at[blocks(0, 15), :])
     left("so", sib_out)
-    left("bo", b_out.at[blocks(0, 12), :])
+    left("bo", tbuf.at[blocks(0, 12), :])
     left("zo", z_out.at[blocks(0, 7), :])
-    left("ao", a_out.at[blocks(0, 3), :])
-    keep.wait()
-    got("g", g_in.at[pl.ds(0, 3)])
-    for j in range(4):
-        oimg[pl.ds((j % 2) * H + (j // 2) * R, R), :] = g_in[j]
-    left("g", g_out.at[pl.ds(0, 3)])
+    left("ao", tbuf.at[blocks(0, 3), :])
+    left("bi", b_inner.at[pl.ds(4, 12)])
+    left("ai", a_inner.at[pl.ds(1, 3)])
+    got("g", rrem.at[0, pl.ds(0, 5 * R), :])
+    put_image(there, g_main_in[...], g_rest_in[...])
+    left("g", g_main.at[0])
+    left("h", g_rest)
     assert (len(send_ids), len(recv_ids)) == (SENDS, RECVS), (len(send_ids), len(recv_ids))
 
 
@@ -432,6 +513,8 @@
             vmem((4, N, 256), BF16),
             vmem((2, N // 2, 128), BF16),
             vmem((R, D), BF16),
+            vmem((R, D), F32),
+            vmem((R, 128), F32),
             vmem((N, D), BF16),
             vmem((N, D), BF16),
             vmem((N, EARLY), BF16),
@@ -442,12 +525,24 @@
             vmem((8 * R, D), BF16),
             vmem((8 * R, D), BF16),
             vmem((8 * R, D), BF16),
-            vmem((N, D), BF16),
-            vmem((N, D), BF16),
-            vmem((4 * R, D), BF16),
-            vmem((4 * R, D), BF16),
-            vmem((4, R, Q), BF16),
-            vmem((4, R, Q), BF16),
+            vmem((16 * H, 512), BF16),
+            vmem((16 * R, 128), BF16),
+            vmem((16 * H, 512), BF16),
+            vmem((16 * R, 128), BF16),
+            vmem((4 * H, 512), BF16),
+            vmem((4 * R, 128), BF16),
+            vmem((4 * H, 512), BF16),
+            vmem((4 * R, 128), BF16),
+            vmem((8 * 128, 256), BF16),
+            vmem((8, 8, 128), F32),
+            vmem((16, 8, 128), F32),
+            vmem((16, 8, 128), F32),
+            vmem((4, 8, 128), F32),
+            vmem((4, 8, 128), F32),
+            vmem((2, H, 256), BF16),
+            vmem((R, 128), BF16),
+            vmem((H, 256), BF16),
+            vmem((R, 128), BF16),
             pltpu.SemaphoreType.DMA((SENDS,)),
             pltpu.SemaphoreType.DMA((RECVS,)),
             pltpu.SemaphoreType.DMA((3,)),

time: 53.5 us -> 52.4 us (0.979)
  Pallas kernels: 50.5 us -> 49.4 us
    pallas_call x1, Pallas kernels: 50.5 us -> 49.4 us  [on_device(): pl.pallas_call(kernel, out_shape=(jax.ShapeDtypeStruct((4 * R, Q), BF16),...]
where the time goes in v4:
time: 52.4 us; the launch traced here: 52.3 us
  Pallas kernels  49.4 us (94%)
  local copies, waits for them, and re-layouts  2.27 us (4%)
  between operations  0.65 us (1%)
    pallas_call x1, Pallas kernels, on_device(): pl.pallas_call(kernel, out_shape=(jax.ShapeDtypeStruct((4 * R, Q), BF16),...  49.4 us
    unnamed x4, local copies, waits for them, and re-layouts  2.27 us

profile of v4, /device:TPU:1, one launch (start us, length us, event | category | flops | bytes accessed | tf_op | source)
XLA Modules:
  0.0 52.3 jit_solution(6301085270805477436)
XLA Ops:
  0.6 49.4 %shard_map.41 = (bf16[192,288]{1,0:T(8,128)(2,1)}, bf16[48,1152]{1,0:T(8,128)(2,1)}) custom-call(bf16[192,288]{1,0:T(8,128)(2,1)} %img.1, bf16[48,1152]{1,0:T(8,128)(2,1)} %txt.1), custom_call_target="tpu_custom_call" | custom-call | flops 4076863488 | bytes 442368 | tf_op jit(solution)/shard_map/pallas_call | solution.py:501
  50.0 0.0 copy-start
  50.0 1.6 %copy.6 = bf16[192,288]{1,0:T(8,128)(2,1)} copy(bf16[192,288]{1,0:T(8,128)(2,1)} %get-tuple-element.4) | data formatting | bytes 221184
  51.7 0.0 copy-done
  51.7 0.6 %copy.7 = bf16[48,1152]{1,0:T(8,128)(2,1)} copy(bf16[48,1152]{1,0:T(8,128)(2,1)S(1)} %copy-done) | data formatting | bytes 221184
Async XLA Ops:
  50.0 1.6 %copy-start = (bf16[48,1152]{1,0:T(8,128)(2,1)S(1)}, bf16[48,1152]{1,0:T(8,128)(2,1)}, u32[]{:S(2)}) copy-start(bf16[48,1152]{1,0:T(8,128)(2,1)} %get-tuple-element.5) | copy-start | bytes 331780

commit v5 on v4

--- a/solution.py
+++ b/solution.py
@@ -355,48 +355,6 @@
     coef_of(6, 2, late)
     coef_of(6, 2, early)
 
-    def send_so(k):
-        rows = blocks(k)
-        sib_out[rows, :] = tp[blocks(OTHER[k]), :].astype(BF16)
-        copy_of("so", ("so", k), sib_out.at[rows, :], sib_in.at[rows, :], "sib").start()
-
-    tp[late[1], :] = text_sums(0, 8, late)
-    for k in (4, 5, 3):
-        send_so(k)
-    tp[early[1], :] += text_sums(6, 2, early)
-    for k in (6, 2, 7, 1, 0):
-        send_so(k)
-    def z_pass(k, to, new):
-        got(("so", k), sib_in.at[blocks(k), :])
-        for p in pieces:
-            rows = rows_of(k, p)
-            total = tp[rows_of(OWN[k], p), :] + sib_in[rows, :].astype(F32)
-            for came in (k,) if k not in (4, 5) else ():
-                place = rows_of(came, p)
-                got(("zo", came, p), z_in.at[place, :])
-                total = total + z_in[place, :].astype(F32)
-            z_out[rows, :] = total.astype(BF16)
-            key = ("zo", new) if new in (0, 8) else ("zo", new, p)
-            slot = 4 if new == 8 else new
-            copy_of("zo", key, z_out.at[rows, :], z_in.at[rows_of(slot, p), :], to).start()
-
-    z_pass(4, "zp", 3)
-    z_pass(5, "zm", 6)
-    ip[second, :] += image_sums(4, 2, late)
-    ip[third, :] = image_sums(6, 2, early) + image_sums(6, 2, late)
-    for d1 in (2, 1, 3, 0):
-        send_b(d1, 2)
-
-    def b_sum(d1):
-        got(("bo", d1), tbuf.at[blocks(0, 3), :])
-        shard = shard_of(d1, 0)
-        for d2 in (1, 2, 3):
-            shard = add_shard(shard, 4 * d2 + d1, b_main_in, b_rest_in)
-        return shard
-
-    def send_a(d1, to):
-        send_shard("ao", "ao", d1, b_sum(d1), a_main, a_rest, a_main_in, a_rest_in, to)
-
     def inner_b():
         lax.fori_loop(0, 8, raw_inner, 0)
         along = lax.dot_general(
@@ -411,6 +369,49 @@
             to = {1: "bp", 2: "b2", 3: "bm"}[d2]
             copy_of("bi", "bi", b_inner.at[four], b_inner_in.at[four], to).start()
 
+    def send_so(k):
+        rows = blocks(k)
+        sib_out[rows, :] = tp[blocks(OTHER[k]), :].astype(BF16)
+        copy_of("so", ("so", k), sib_out.at[rows, :], sib_in.at[rows, :], "sib").start()
+
+    tp[late[1], :] = text_sums(0, 8, late)
+    for k in (4, 5, 3):
+        send_so(k)
+    tp[early[1], :] += text_sums(6, 2, early)
+    for k in (6, 2, 7, 1, 0):
+        send_so(k)
+    def z_pass(*hops):
+        for k, to, new in hops:
+            got(("so", k), sib_in.at[blocks(k), :])
+        for p in pieces:
+            for k, to, new in hops:
+                rows = rows_of(k, p)
+                total = tp[rows_of(OWN[k], p), :] + sib_in[rows, :].astype(F32)
+                if k not in (4, 5):
+                    got(("zo", k, p), z_in.at[rows, :])
+                    total = total + z_in[rows, :].astype(F32)
+                z_out[rows, :] = total.astype(BF16)
+                key = ("zo", new) if new in (0, 8) else ("zo", new, p)
+                slot = 4 if new == 8 else new
+                copy_of("zo", key, z_out.at[rows, :], z_in.at[rows_of(slot, p), :], to).start()
+
+    z_pass((4, "zp", 3), (5, "zm", 6))
+    ip[second, :] += image_sums(4, 2, late)
+    ip[third, :] = image_sums(6, 2, early) + image_sums(6, 2, late)
+    inner_b()
+    for d1 in (2, 1, 3, 0):
+        send_b(d1, 2)
+
+    def b_sum(d1):
+        got(("bo", d1), tbuf.at[blocks(0, 3), :])
+        shard = shard_of(d1, 0)
+        for d2 in (1, 2, 3):
+            shard = add_shard(shard, 4 * d2 + d1, b_main_in, b_rest_in)
+        return shard
+
+    def send_a(d1, to):
+        send_shard("ao", "ao", d1, b_sum(d1), a_main, a_rest, a_main_in, a_rest_in, to)
+
     def inner_sum(d1):
         return inner_slots[slot_of(d1, 0)] + b_inner_in[4 + d1] + b_inner_in[8 + d1] + b_inner_in[12 + d1]
 
@@ -420,16 +421,13 @@
             a_inner[d1] = inner_sum(d1)
             copy_of("ai", "ai", a_inner.at[d1], a_inner_in.at[d1], to).start()
 
-    z_pass(3, "zp", 2)
-    z_pass(6, "zm", 7)
-    inner_b()
+    z_pass((3, "zp", 2), (6, "zm", 7))
     send_a(2, "a2")
-    z_pass(2, "zp", 1)
-    z_pass(7, "zm", 8)
+    z_pass((2, "zp", 1), (7, "zm", 8))
     send_a(1, "ap")
     send_a(3, "am")
     inner_a()
-    z_pass(1, "zp", 0)
+    z_pass((1, "zp", 0))
 
     def back_norm(unit_rows, scale, inner, direction):
         return scale * (direction - unit_rows * inner)
@@ -448,16 +446,6 @@
     inner_i = scale_i * jnp.transpose(jnp.broadcast_to(along[:1], (128, 128)))[:H, :1]
     inner_rest = jnp.where(left_side, inner_i[:R], inner_i[R:])
 
-    got(("so", 0), sib_in.at[blocks(0), :])
-    got(("zo", 0), z_in.at[blocks(0), :])
-    got(("zo", 8), z_in.at[blocks(4), :])
-    direction = tp[blocks(0), :] + sib_in[blocks(0), :].astype(F32)
-    direction = direction + z_in[blocks(0), :].astype(F32) + z_in[blocks(4), :].astype(F32)
-    text_unit, text_scale = tunit[...], tscales[:, :1]
-    text_inner = jnp.sum(text_unit * direction, axis=-1, keepdims=True)
-    text_grad = back_norm(text_unit, text_scale, text_inner, direction)
-    otxt[...] = jnp.concatenate([quarter(text_grad, j) for j in range(4)], axis=1).astype(BF16)
-
     shard = b_sum(0)
     got("ao", tbuf.at[blocks(0, 3), :])
     for d1 in (1, 2, 3):
@@ -477,6 +465,16 @@
         oimg[rows, pl.ds(256, 32)] = jnp.concatenate([low, high], axis=0).astype(BF16)
 
     put_image(here, g_main[c], g_rest[...])
+
+    got(("so", 0), sib_in.at[blocks(0), :])
+    got(("zo", 0), z_in.at[blocks(0), :])
+    got(("zo", 8), z_in.at[blocks(4), :])
+    direction = tp[blocks(0), :] + sib_in[blocks(0), :].astype(F32)
+    direction = direction + z_in[blocks(0), :].astype(F32) + z_in[blocks(4), :].astype(F32)
+    text_unit, text_scale = tunit[...], tscales[:, :1]
+    text_inner = jnp.sum(text_unit * direction, axis=-1, keepdims=True)
+    text_grad = back_norm(text_unit, text_scale, text_inner, direction)
+    otxt[...] = jnp.concatenate([quarter(text_grad, j) for j in range(4)], axis=1).astype(BF16)
 
     left("x", rmain.at[0, pl.ds(0, H), :])
     left("y", xrem)
@@ -496,9 +494,20 @@
     assert (len(send_ids), len(recv_ids)) == (SENDS, RECVS), (len(send_ids), len(recv_ids))
 
 
+def hand_out(image_grad, text_grad, oimg, otxt, sems):
+    copies = [
+        pltpu.make_async_copy(image_grad, oimg, sems.at[0]),
+        pltpu.make_async_copy(text_grad, otxt, sems.at[1]),
+    ]
+    for copy in copies:
+        copy.start()
+    for copy in copies:
+        copy.wait()
+
+
 def on_device(image_features, text_features):
     vmem = pltpu.VMEM
-    return pl.pallas_call(
+    image_grad, text_grad = pl.pallas_call(
         kernel,
         out_shape=(
             jax.ShapeDtypeStruct((4 * R, Q), BF16),
@@ -554,6 +563,16 @@
             flops=6 * N * N * D, bytes_accessed=8 * R * D, transcendentals=N * N
         ),
     )(image_features, text_features)
+    return pl.pallas_call(
+        hand_out,
+        out_shape=(
+            jax.ShapeDtypeStruct((4 * R, Q), BF16),
+            jax.ShapeDtypeStruct((R, D), BF16),
+        ),
+        in_specs=[pl.BlockSpec(memory_space=pltpu.VMEM)] * 2,
+        out_specs=[pl.BlockSpec(memory_space=pltpu.HBM)] * 2,
+        scratch_shapes=[pltpu.SemaphoreType.DMA((2,))],
+    )(image_grad, text_grad)
 
 
 def solution(mesh):

time: 52.4 us -> 50.7 us (0.968)
  local copies, waits for them, and re-layouts: 2.27 us -> 0 us
  Pallas kernels: 49.4 us -> 50 us
    unnamed x4 -> x0, local copies, waits for them, and re-layouts: 2.27 us -> none
    pallas_call x0 -> x1, Pallas kernels: none -> 1.68 us  [on_device(): pl.pallas_call(hand_out, out_shape=(jax.ShapeDtypeStruct((4 * R, Q), BF16...]
    pallas_call x1, Pallas kernels: 49.4 us -> 48.3 us  [on_device(): pl.pallas_call(kernel, out_shape=(jax.ShapeDtypeStruct((4 * R, Q), BF16),...]
where the time goes in v5:
time: 50.7 us; the launch traced here: 50.6 us
  Pallas kernels  50 us (99%)
  between operations  0.64 us (1%)
    pallas_call x1, Pallas kernels, on_device(): pl.pallas_call(kernel, out_shape=(jax.ShapeDtypeStruct((4 * R, Q), BF16),...  48.3 us
    pallas_call x1, Pallas kernels, on_device(): pl.pallas_call(hand_out, out_shape=(jax.ShapeDtypeStruct((4 * R, Q), BF16...  1.68 us

profile of v5, /device:TPU:1, one launch (start us, length us, event | category | flops | bytes accessed | tf_op | source)
XLA Modules:
  0.0 50.6 jit_solution(10318080035321543961)
XLA Ops:
  0.6 48.3 %shard_map.41 = (bf16[192,288]{1,0:T(8,128)(2,1)}, bf16[48,1152]{1,0:T(8,128)(2,1)}) custom-call(bf16[192,288]{1,0:T(8,128)(2,1)} %img.1, bf16[48,1152]{1,0:T(8,128)(2,1)} %txt.1), custom_call_target="tpu_custom_call" | custom-call | flops 4076863488 | bytes 442368 | tf_op jit(solution)/shard_map/pallas_call | solution.py:510
  48.9 1.7 %shard_map.42 = (bf16[192,288]{1,0:T(8,128)(2,1)}, bf16[48,1152]{1,0:T(8,128)(2,1)}) custom-call(bf16[192,288]{1,0:T(8,128)(2,1)} %get-tuple-element.4.image_grad, bf16[48,1152]{1,0:T(8,128)(2,1)} %get-tuple-element.5.text_grad), custom_call_target="tpu_custom_call" | custom-call | tf_op jit(solution)/shard_map/pallas_call | solution.py:566

commit v6 on v5

--- a/solution.py
+++ b/solution.py
@@ -142,9 +142,6 @@
     rmain[grp, pl.ds(4 * H, H), :] = ximg[here, :256]
     pl.semaphore_wait(barrier, len(GREETED))
 
-    copy_of("x", "x", ximg.at[there, pl.ds(0, 256)], rmain.at[grp, pl.ds(4 * H, H), :], "sib").start()
-    copy_of("y", "x", xrem, srem, "sib").start()
-
     def send_t(to, slot, new, piece):
         key = ("t", new) if new in (3, 4, 5) else ("t", new, piece)
         src, dst = rows_of(OWN[slot], piece), rows_of(OWN[new], piece)
@@ -158,6 +155,9 @@
     for p in pieces:
         send_t("zm", 0, 1, p)
         send_t("zp", 0, 7, p)
+
+    copy_of("x", "x", ximg.at[there, pl.ds(0, 256)], rmain.at[grp, pl.ds(4 * H, H), :], "sib").start()
+    copy_of("y", "x", xrem, srem, "sib").start()
     send_s(0)
 
     def slot_of(d1, d2):
@@ -198,8 +198,8 @@
     rrem[xh, pl.ds(4 * R, R), :] = (rest_here + srem[...].astype(F32)).astype(BF16)
     send_i("am", (0, 0), (1, 0), ("i", 1, 0))
     send_i("ap", (0, 0), (3, 0), ("i", 3, 0))
+    near_b(0)
     send_i("a2", (0, 0), (2, 0), ("i", 2, 0))
-    near_b(0)
 
     def ring_t(new_m, new_p):
         for p in pieces:
@@ -339,7 +339,6 @@
     normalised(4, 2)
     coef_of(4, 2, early)
     late_t(4)
-    tp[early[1], :] = text_sums(0, 6, early)
     ip[second, :] = image_sums(4, 2, early)
 
     got("s late", tbuf.at[blocks(0, 3), :])
@@ -377,7 +376,7 @@
     tp[late[1], :] = text_sums(0, 8, late)
     for k in (4, 5, 3):
         send_so(k)
-    tp[early[1], :] += text_sums(6, 2, early)
+    tp[early[1], :] = text_sums(0, 8, early)
     for k in (6, 2, 7, 1, 0):
         send_so(k)
     def z_pass(*hops):

time: 50.7 us -> 50.7 us (level)
  no operation moved by 1% of the time
where the time goes in v6:
time: 50.7 us; the launch traced here: 50.5 us
  Pallas kernels  49.9 us (98%)
  between operations  0.64 us (1%)
    pallas_call x1, Pallas kernels, on_device(): pl.pallas_call(kernel, out_shape=(jax.ShapeDtypeStruct((4 * R, Q), BF16),...  48.2 us
    pallas_call x1, Pallas kernels, on_device(): pl.pallas_call(hand_out, out_shape=(jax.ShapeDtypeStruct((4 * R, Q), BF16...  1.68 us

profile of v6, /device:TPU:1, one launch (start us, length us, event | category | flops | bytes accessed | tf_op | source)
XLA Modules:
  0.0 50.5 jit_solution(3367860838759853430)
XLA Ops:
  0.6 48.2 %shard_map.41 = (bf16[192,288]{1,0:T(8,128)(2,1)}, bf16[48,1152]{1,0:T(8,128)(2,1)}) custom-call(bf16[192,288]{1,0:T(8,128)(2,1)} %img.1, bf16[48,1152]{1,0:T(8,128)(2,1)} %txt.1), custom_call_target="tpu_custom_call" | custom-call | flops 4076863488 | bytes 442368 | tf_op jit(solution)/shard_map/pallas_call | solution.py:509
  48.9 1.7 %shard_map.42 = (bf16[192,288]{1,0:T(8,128)(2,1)}, bf16[48,1152]{1,0:T(8,128)(2,1)}) custom-call(bf16[192,288]{1,0:T(8,128)(2,1)} %get-tuple-element.4.image_grad, bf16[48,1152]{1,0:T(8,128)(2,1)} %get-tuple-element.5.text_grad), custom_call_target="tpu_custom_call" | custom-call | tf_op jit(solution)/shard_map/pallas_call | solution.py:565

commit v7 on v6

--- a/solution.py
+++ b/solution.py
@@ -327,7 +327,7 @@
         for d2 in (1, 3):
             if d1 not in FORWARD or d2 != (1 if d1 in VIA_P else 3):
                 got_i(("i", d1, d2))
-    first, second, third = pl.ds(0, 4 * H), pl.ds(4 * H, 2 * H), pl.ds(6 * H, 2 * H)
+    first, second = pl.ds(0, 4 * H), pl.ds(4 * H, 4 * H)
     normalised(0, 4)
     got("s early", tbuf.at[blocks(0, 5), :])
     coef_of(0, 4, early)
@@ -339,7 +339,6 @@
     normalised(4, 2)
     coef_of(4, 2, early)
     late_t(4)
-    ip[second, :] = image_sums(4, 2, early)
 
     got("s late", tbuf.at[blocks(0, 3), :])
     coef_of(0, 4, late)
@@ -395,8 +394,7 @@
                 copy_of("zo", key, z_out.at[rows, :], z_in.at[rows_of(slot, p), :], to).start()
 
     z_pass((4, "zp", 3), (5, "zm", 6))
-    ip[second, :] += image_sums(4, 2, late)
-    ip[third, :] = image_sums(6, 2, early) + image_sums(6, 2, late)
+    ip[second, :] = image_sums(4, 4, early) + image_sums(4, 4, late)
     inner_b()
     for d1 in (2, 1, 3, 0):
         send_b(d1, 2)

time: 50.7 us -> 50.7 us (level)
  no operation moved by 1% of the time
where the time goes in v7:
time: 50.7 us; the launch traced here: 50.5 us
  Pallas kernels  49.9 us (98%)
  between operations  0.64 us (1%)
    pallas_call x1, Pallas kernels, on_device(): pl.pallas_call(kernel, out_shape=(jax.ShapeDtypeStruct((4 * R, Q), BF16),...  48.2 us
    pallas_call x1, Pallas kernels, on_device(): pl.pallas_call(hand_out, out_shape=(jax.ShapeDtypeStruct((4 * R, Q), BF16...  1.68 us

profile of v7, /device:TPU:1, one launch (start us, length us, event | category | flops | bytes accessed | tf_op | source)
XLA Modules:
  0.0 50.5 jit_solution(733418860182397542)
XLA Ops:
  0.6 48.2 %shard_map.41 = (bf16[192,288]{1,0:T(8,128)(2,1)}, bf16[48,1152]{1,0:T(8,128)(2,1)}) custom-call(bf16[192,288]{1,0:T(8,128)(2,1)} %img.1, bf16[48,1152]{1,0:T(8,128)(2,1)} %txt.1), custom_call_target="tpu_custom_call" | custom-call | flops 4076863488 | bytes 442368 | tf_op jit(solution)/shard_map/pallas_call | solution.py:507
  48.9 1.7 %shard_map.42 = (bf16[192,288]{1,0:T(8,128)(2,1)}, bf16[48,1152]{1,0:T(8,128)(2,1)}) custom-call(bf16[192,288]{1,0:T(8,128)(2,1)} %get-tuple-element.4.image_grad, bf16[48,1152]{1,0:T(8,128)(2,1)} %get-tuple-element.5.text_grad), custom_call_target="tpu_custom_call" | custom-call | tf_op jit(solution)/shard_map/pallas_call | solution.py:563

commit v8 on v7

--- a/solution.py
+++ b/solution.py
@@ -177,6 +177,19 @@
         dst = pl.ds(pl.multiple_of(goes * R, 16), R)
         copy_of("i", key, rrem.at[half, src, :], rrem.at[half, dst, :], to).start()
 
+    first_hops = (
+        ("am", (1, 0), ("i", 1, 0)), ("ap", (3, 0), ("i", 3, 0)),
+        ("bm", (0, 1), ("i", 0, 1)), ("bp", (0, 3), ("i", 0, 3)), ("a2", (2, 0), ("i", 2, 0)),
+    )
+
+    def send_quarter(to, target, key, q):
+        dst = pl.ds(pl.multiple_of(slot_of(*target) * H, 32), H)
+        copy_of("i", key, rmain.at[q, pl.ds(4 * H, H), :], rmain.at[q, dst, :], to).start()
+
+    def send_rest(to, target, key):
+        dst = pl.ds(pl.multiple_of(slot_of(*target) * R, 16), R)
+        copy_of("i", key, rrem.at[xh, blocks(4), :], rrem.at[xh, dst, :], to).start()
+
     def got_i(key):
         got(key, tbuf.at[blocks(0), :])
 
@@ -194,12 +207,13 @@
             got_i(("i", d1, 3))
             send_i("bp", (d1, 3), (d1, 2), ("i", d1, 2))
 
+    for hop in first_hops:
+        send_quarter(*hop, grp)
     got("x", rrem.at[0, pl.ds(0, 5 * R), :])
     rrem[xh, pl.ds(4 * R, R), :] = (rest_here + srem[...].astype(F32)).astype(BF16)
-    send_i("am", (0, 0), (1, 0), ("i", 1, 0))
-    send_i("ap", (0, 0), (3, 0), ("i", 3, 0))
-    near_b(0)
-    send_i("a2", (0, 0), (2, 0), ("i", 2, 0))
+    for hop in first_hops:
+        send_quarter(*hop, 2 * xh + 1 - c)
+        send_rest(*hop)
 
     def ring_t(new_m, new_p):
         for p in pieces:

time: 50.7 us -> 50.7 us (level)
  no operation moved by 1% of the time
where the time goes in v8:
time: 50.7 us; the launch traced here: 50.6 us
  Pallas kernels  50 us (99%)
  between operations  0.64 us (1%)
    pallas_call x1, Pallas kernels, on_device(): pl.pallas_call(kernel, out_shape=(jax.ShapeDtypeStruct((4 * R, Q), BF16),...  48.3 us
    pallas_call x1, Pallas kernels, on_device(): pl.pallas_call(hand_out, out_shape=(jax.ShapeDtypeStruct((4 * R, Q), BF16...  1.68 us

profile of v8, /device:TPU:1, one launch (start us, length us, event | category | flops | bytes accessed | tf_op | source)
XLA Modules:
  0.0 50.6 jit_solution(14690719791656001753)
XLA Ops:
  0.6 48.3 %shard_map.41 = (bf16[192,288]{1,0:T(8,128)(2,1)}, bf16[48,1152]{1,0:T(8,128)(2,1)}) custom-call(bf16[192,288]{1,0:T(8,128)(2,1)} %img.1, bf16[48,1152]{1,0:T(8,128)(2,1)} %txt.1), custom_call_target="tpu_custom_call" | custom-call | flops 4076863488 | bytes 442368 | tf_op jit(solution)/shard_map/pallas_call | solution.py:521
  48.9 1.7 %shard_map.42 = (bf16[192,288]{1,0:T(8,128)(2,1)}, bf16[48,1152]{1,0:T(8,128)(2,1)}) custom-call(bf16[192,288]{1,0:T(8,128)(2,1)} %get-tuple-element.4.image_grad, bf16[48,1152]{1,0:T(8,128)(2,1)} %get-tuple-element.5.text_grad), custom_call_target="tpu_custom_call" | custom-call | tf_op jit(solution)/shard_map/pallas_call | solution.py:577
